TPU v7x, 256 devices: a whole 4x4x8 slice. The times are simulated.
256 devices in a mesh: depth: 2 (over core), row: 8 (over z), col: 16 (over y, x).
Axes of the slice: x: 4, y: 4, z: 8, core: 2. Of those that a mesh axis runs over, the one named last changes fastest.
Arguments:
- rhs: float32 [2, 4096, 256], P('depth', ('row', 'col')), may hold values from -8 to 8
- factor_blocks: float32 [2, 8, 16, 512, 4096], P('depth', 'row', 'col'), may hold values from -0.1875 to 0.1875
- block_rows: int32 [2, 8, 16, 512], P('depth', 'row', 'col'), may hold values from 0 to 511
- block_cols: int32 [2, 8, 16, 512], P('depth', 'row', 'col'), may hold values from 0 to 255
- diag_inverse: float32 [2, 4096, 4096], P('depth', ('row', 'col')), may hold values from -0.225 to 1.225
- coupling: float32 [2, 128, 4096], P('depth', ('row', 'col')), may hold values from -2 to 2
Outputs:
- solution: float32 [2, 4096, 256], P('depth', ('row', 'col'))
All inputs are finite; a program needn't handle non-finite values.
Results may differ from a plain program's by a relative error of at most 0.00015.
Values sent between devices are 32-bit elements; how exact they have to be, the bound alone decides.
A program may use at most 128 MiB of HBM per device.

v0:
```python
import jax
import jax.numpy as jnp
from jax import lax
from jax.sharding import PartitionSpec as P

BLOCK = 64
NZ = 512


def passed_along(block, axis, distance):
    devices = range(lax.axis_size(axis))
    route = [(i - distance, i) for i in devices if i - distance in devices]
    return lax.ppermute(block, axis, route)


def mix(mats, vecs):
    count = vecs.shape[0]
    shaped = vecs.reshape(count, -1, BLOCK)
    out = jnp.einsum("kab,krb->kra", mats, shaped, precision=lax.Precision.HIGHEST)
    return out.reshape(count, -1)


def mix_back(mats, vecs):
    count = vecs.shape[0]
    shaped = vecs.reshape(count, -1, BLOCK)
    out = jnp.einsum("kab,kra->krb", mats, shaped, precision=lax.Precision.HIGHEST)
    return out.reshape(count, -1)


def pass_face(values, offset):
    return passed_along(values, "depth", offset)


def per_device(rhs, factor_blocks, block_rows, block_cols, diag_inverse, coupling):
    nbf = rhs.shape[1]
    ncol = lax.axis_size("col")
    nrow = lax.axis_size("row")
    start = rhs[0]
    mats = factor_blocks[0, 0, 0].reshape(NZ, BLOCK, BLOCK)
    targets = block_rows[0, 0, 0]
    sources = block_cols[0, 0, 0]
    couple_mat = coupling[0, 0:1].reshape(1, BLOCK, BLOCK)
    diag_own = diag_inverse[0].reshape(nbf, BLOCK, BLOCK)

    def solve(field):
        columns = lax.all_gather(field, "row", axis=0, tiled=True)
        term = jax.ops.segment_sum(mix(mats, columns[sources]), targets, num_segments=ncol * nbf)
        summed = lax.psum_scatter(term, "col", scatter_dimension=0, tiled=True) + field
        own = mix(diag_own, summed)
        scaled = lax.all_gather(own, "col", axis=0, tiled=True)
        back = jax.ops.segment_sum(
            mix_back(mats, scaled[targets]), sources, num_segments=nrow * nbf
        )
        return lax.psum_scatter(back, "row", scatter_dimension=0, tiled=True) + own

    field = start
    current = solve(field)
    arrived = pass_face(current[nbf - 1 : nbf], 1)
    pushed = mix(couple_mat, arrived)
    field = start.at[0:1].add(-pushed)
    current = solve(field)
    pulled = mix_back(couple_mat, current[0:1])
    arrived = pass_face(pulled, -1)
    current = solve(field.at[nbf - 1 : nbf].add(-arrived))
    return current[None]


def solution(mesh):
    placed = (
        P("depth", ("row", "col"), None),
        P("depth", "row", "col", None, None),
        P("depth", "row", "col", None),
        P("depth", "row", "col", None),
        P("depth", ("row", "col"), None),
        P("depth", ("row", "col"), None),
    )
    return jax.shard_map(
        per_device,
        mesh=mesh,
        in_specs=placed,
        out_specs=P("depth", ("row", "col"), None),
        check_vma=False,
    )
```

profile of v0, /device:TPU:32, one launch (start us, length us, event | category | flops | bytes accessed | tf_op | source)
XLA Modules:
  0.0 720.6 jit_solution(5334650763224802197)
XLA Ops:
  7.3 9.0 %copy.8 = f32[1,1,1,512,4096]{3,4,2,1,0:T(8,128)} copy(f32[1,1,1,512,4096]{4,3,2,1,0:T(8,128)} %param.11) | data formatting | bytes 16777216 | tf_op args[1]
  16.3 16.3 %copy.10 = f32[512,64,64]{2,1,0:T(8,128)} copy(f32[512,64,64]{0,2,1:T(8,128)} %bitcast.51) | data formatting | bytes 16777216 | tf_op jit(solution)/shard_map/reshape;squeeze | solution.py:39
  32.6 27.6 %all-gather = f32[1,256,256]{2,1,0:T(8,128)S(1)} all-gather(f32[1,32,256]{2,1,0:T(8,128)S(1)} %copy.41), channel_id=2, replica_groups=mesh['depth'=2,'row'=8,'col'=16] {'row'}, dimensions={1}, use_global_device_ids=true | all-gather | bytes 294912 | tf_op jit(solution)/shard_map/all_gather | solution.py:46
  60.2 1.6 gather_fusion
  62.4 29.0 %fusion.13 = f32[512,4,64]{2,1,0:T(4,128)S(1)} fusion(f32[512,4,64]{2,1,0:T(4,128)S(1)} %copy.9, f32[512,64,64]{2,1,0:T(8,128)} %copy.10), kind=kOutput, calls=%fused_computation.36 | convolution fusion | flops 100663296 | bytes 9437184 | tf_op jit(solution)/shard_map/kab,krb->kra/dot_general | solution.py:19
  91.9 4.1 scatter_custom_fusion
  96.8 76.6 %reduce-scatter.7.cloned.1.call-done = f32[32,256]{1,0:T(8,128)} async-done(((f32[512,256]{1,0:T(8,128)}), f32[32,256]{1,0:T(8,128)}) %reduce-scatter.7.cloned.1.call-update) | async-done | bytes 32784 | tf_op jit(solution)/shard_map/reduce_scatter | solution.py:48
  174.2 1.7 fusion.14
  176.1 23.3 %all_gather.19 = f32[512,256]{1,0:T(8,128)S(1)} all-gather(f32[32,256]{1,0:T(8,128)S(1)} %reshape.212), channel_id=1, replica_groups=mesh['depth'=2,'row'=8,'col'=16] {'col'}, dimensions={0}, use_global_device_ids=true | all-gather | bytes 557056 | tf_op jit(solution)/shard_map/all_gather | solution.py:50
  199.4 1.6 gather_fusion.1
  201.6 17.1 %fusion.15 = f32[512,4,64]{2,1,0:T(4,128)S(1)} fusion(f32[512,4,64]{2,1,0:T(4,128)S(1)} %copy.14, f32[512,64,64]{2,1,0:T(8,128)} %copy.10), kind=kOutput, calls=%fused_computation.38 | convolution fusion | flops 100663296 | bytes 9437184 | tf_op jit(solution)/shard_map/kab,kra->krb/dot_general | solution.py:26
  219.2 4.0 scatter_custom_fusion.1
  223.3 35.0 %reduce-scatter.9.cloned.1.call-done = f32[32,256]{1,0:T(8,128)} async-done(((f32[256,256]{1,0:T(8,128)}), f32[32,256]{1,0:T(8,128)}) %reduce-scatter.9.cloned.1.call-update) | async-done | bytes 32784 | tf_op jit(solution)/shard_map/reduce_scatter | solution.py:54
  262.6 25.3 %all_gather.20 = f32[256,256]{1,0:T(8,128)S(1)} all-gather(f32[32,256]{1,0:T(8,128)S(1)} %scatter-add.54), channel_id=1, replica_groups=mesh['depth'=2,'row'=8,'col'=16] {'row'}, dimensions={0}, use_global_device_ids=true | all-gather | bytes 294912 | tf_op jit(solution)/shard_map/all_gather | solution.py:46
  290.1 29.0 %fusion.16 = f32[512,4,64]{2,1,0:T(4,128)S(1)} fusion(f32[512,4,64]{2,1,0:T(4,128)S(1)} %copy.19, f32[512,64,64]{2,1,0:T(8,128)} %copy.10), kind=kOutput, calls=%fused_computation.39 | convolution fusion | flops 100663296 | bytes 9437184 | tf_op jit(solution)/shard_map/kab,krb->kra/dot_general | solution.py:19
  319.6 4.1 scatter_custom_fusion.2
  323.9 76.4 %reduce-scatter.11.cloned.1.call-done = f32[32,256]{1,0:T(8,128)} async-done(((f32[512,256]{1,0:T(8,128)}), f32[32,256]{1,0:T(8,128)}) %reduce-scatter.11.cloned.1.call-update) | async-done | bytes 32784 | tf_op jit(solution)/shard_map/reduce_scatter | solution.py:48
  401.2 1.7 fusion.17
  403.1 23.3 %all_gather.21 = f32[512,256]{1,0:T(8,128)S(1)} all-gather(f32[32,256]{1,0:T(8,128)S(1)} %reshape.220), channel_id=1, replica_groups=mesh['depth'=2,'row'=8,'col'=16] {'col'}, dimensions={0}, use_global_device_ids=true | all-gather | bytes 557056 | tf_op jit(solution)/shard_map/all_gather | solution.py:50
  428.5 17.1 %fusion.18 = f32[512,4,64]{2,1,0:T(4,128)S(1)} fusion(f32[512,4,64]{2,1,0:T(4,128)S(1)} %copy.24, f32[512,64,64]{2,1,0:T(8,128)} %copy.10), kind=kOutput, calls=%fused_computation.41 | convolution fusion | flops 100663296 | bytes 9437184 | tf_op jit(solution)/shard_map/kab,kra->krb/dot_general | solution.py:26
  446.2 4.0 scatter_custom_fusion.3
  450.3 35.0 %reduce-scatter.13.cloned.1.call-done = f32[32,256]{1,0:T(8,128)} async-done(((f32[256,256]{1,0:T(8,128)}), f32[32,256]{1,0:T(8,128)}) %reduce-scatter.13.cloned.1.call-update) | async-done | bytes 32784 | tf_op jit(solution)/shard_map/reduce_scatter | solution.py:54
  487.6 1.7 collective-permute-done.1
  489.3 25.0 %all_gather.22 = f32[256,256]{1,0:T(8,128)S(1)} all-gather(f32[32,256]{1,0:T(8,128)S(1)} %scatter-add.57), channel_id=1, replica_groups=mesh['depth'=2,'row'=8,'col'=16] {'row'}, dimensions={0}, use_global_device_ids=true | all-gather | bytes 294912 | tf_op jit(solution)/shard_map/all_gather | solution.py:46
  516.5 29.0 %fusion.20 = f32[512,4,64]{2,1,0:T(4,128)S(1)} fusion(f32[512,4,64]{2,1,0:T(4,128)S(1)} %copy.29, f32[512,64,64]{2,1,0:T(8,128)} %copy.10), kind=kOutput, calls=%fused_computation.43 | convolution fusion | flops 100663296 | bytes 9437184 | tf_op jit(solution)/shard_map/kab,krb->kra/dot_general | solution.py:19
  546.0 4.1 scatter_custom_fusion.4
  550.4 76.6 %reduce-scatter.15.cloned.1.call-done = f32[32,256]{1,0:T(8,128)} async-done(((f32[512,256]{1,0:T(8,128)}), f32[32,256]{1,0:T(8,128)}) %reduce-scatter.15.cloned.1.call-update) | async-done | bytes 32784 | tf_op jit(solution)/shard_map/reduce_scatter | solution.py:48
  627.9 1.7 fusion.21
  629.7 23.3 %all_gather.23 = f32[512,256]{1,0:T(8,128)S(1)} all-gather(f32[32,256]{1,0:T(8,128)S(1)} %reshape.228), channel_id=1, replica_groups=mesh['depth'=2,'row'=8,'col'=16] {'col'}, dimensions={0}, use_global_device_ids=true | all-gather | bytes 557056 | tf_op jit(solution)/shard_map/all_gather | solution.py:50
  655.2 17.1 %fusion.22 = f32[512,4,64]{2,1,0:T(4,128)S(1)} fusion(f32[512,4,64]{2,1,0:T(4,128)S(1)} %copy.34, f32[512,64,64]{2,1,0:T(8,128)} %copy.10), kind=kOutput, calls=%fused_computation.45 | convolution fusion | flops 100663296 | bytes 9437184 | tf_op jit(solution)/shard_map/kab,kra->krb/dot_general | solution.py:26
  672.9 4.0 scatter_custom_fusion.5
  676.9 35.1 %reduce-scatter.17.cloned.1.call-done = f32[32,256]{1,0:T(8,128)} async-done(((f32[256,256]{1,0:T(8,128)}), f32[32,256]{1,0:T(8,128)}) %reduce-scatter.17.cloned.1.call-update) | async-done | bytes 32784 | tf_op jit(solution)/shard_map/reduce_scatter | solution.py:54
  (83 shorter events, 26.1 us)
Async XLA Ops:
  6.5 166.8 %reduce-scatter.7.cloned.1.call-start = ((), (), s32[]{:S(2)}) async-start(), calls=%async_computation.6 | async-start | bytes 557056 | tf_op jit(solution)/shard_map/reduce_scatter | solution.py:48
  16.3 43.9 %copy-start.3 = (s32[1,1,1,512]{3,2,1,0:T(1,128)S(1)}, s32[1,1,1,512]{3,2,1,0:T(1,128)}, u32[]{:S(2)}) copy-start(s32[1,1,1,512]{3,2,1,0:T(1,128)} %param.13) | copy-start | bytes 6148
  32.6 59.4 %copy-start.2 = (s32[1,1,1,512]{3,2,1,0:T(1,128)S(1)}, s32[1,1,1,512]{3,2,1,0:T(1,128)}, u32[]{:S(2)}) copy-start(s32[1,1,1,512]{3,2,1,0:T(1,128)} %param.12) | copy-start | bytes 6148
  32.6 63.8 %copy-start = (f32[1,32,4096]{2,1,0:T(8,128)S(1)}, f32[1,32,4096]{2,1,0:T(8,128)}, u32[]{:S(2)}) copy-start(f32[1,32,4096]{2,1,0:T(8,128)} %param.14) | copy-start | bytes 1572868
  96.0 164.7 %copy-start.1 = (f32[1,1,4096]{2,1,0:T(1,128)S(1)}, f32[1,1,4096]{2,1,0:T(1,128)}, u32[]{:S(2)}) copy-start(f32[1,1,4096]{2,1,0:T(1,128)} %param.15) | copy-start | bytes 49156
  96.0 162.2 %reduce-scatter.9.cloned.1.call-start = ((), (), s32[]{:S(2)}) async-start(), calls=%async_computation.7 | async-start | bytes 294912 | tf_op jit(solution)/shard_map/reduce_scatter | solution.py:54
  223.2 177.1 %reduce-scatter.11.cloned.1.call-start = ((), (), s32[]{:S(2)}) async-start(), calls=%async_computation.8 | async-start | bytes 557056 | tf_op jit(solution)/shard_map/reduce_scatter | solution.py:48
  259.0 2.6 collective-permute-start
  323.7 161.5 %reduce-scatter.13.cloned.1.call-start = ((), (), s32[]{:S(2)}) async-start(), calls=%async_computation.9 | async-start | bytes 294912 | tf_op jit(solution)/shard_map/reduce_scatter | solution.py:54
  450.2 176.8 %reduce-scatter.15.cloned.1.call-start = ((), (), s32[]{:S(2)}) async-start(), calls=%async_computation.10 | async-start | bytes 557056 | tf_op jit(solution)/shard_map/reduce_scatter | solution.py:48
  486.3 3.0 collective-permute-start.1
  550.1 161.8 %reduce-scatter.17.cloned.1.call-start = ((), (), s32[]{:S(2)}) async-start(), calls=%async_computation.11 | async-start | bytes 294912 | tf_op jit(solution)/shard_map/reduce_scatter | solution.py:54
Sparse Core Ops, SparseCore 0:
  96.2 77.1 reduce-scatter.6
  223.4 34.8 reduce-scatter.8
  323.8 76.5 reduce-scatter.10
  450.3 34.8 reduce-scatter.12
  550.3 76.6 reduce-scatter.14
  677.0 34.8 reduce-scatter.16
where the time goes:
time: 731 us; the launch traced here: 721 us
  waiting for transfers between devices  336 us (46%)
  blocking collectives  148 us (20%)
  matrix products  144 us (20%)
  local copies, waits for them, and re-layouts  44.2 us (6%)
  other arithmetic  30.6 us (4%)
  between operations  14.3 us (2%)
    reduce_scatter x3, waiting for transfers between devices, solve(): lax.psum_scatter(term, 'col', scatter_dimension=0, tiled=True) + field  230 us
    reduce_scatter x3, waiting for transfers between devices, solve(): return lax.psum_scatter(back, 'row', scatter_dimension=0, tiled=True) + own  105 us
    dot_general x7, matrix products, mix(): jnp.einsum('kab,krb->kra', mats, shaped, precision=lax.Precision.HIGHEST)  92.2 us
    all_gather x3, blocking collectives, solve(): columns = lax.all_gather(field, 'row', axis=0, tiled=True)  78 us
    all_gather x3, blocking collectives, solve(): scaled = lax.all_gather(own, 'col', axis=0, tiled=True)  69.9 us
    dot_general x4, matrix products, mix_back(): jnp.einsum('kab,kra->krb', mats, shaped, precision=lax.Precision.HIGHEST)  51.5 us
    another operation x1, local copies, waits for them, and re-layouts, per_device(): mats = factor_blocks[0, 0, 0].reshape(NZ, BLOCK, BLOCK)  16.3 us
  transfers between devices with their start and end apart: 8, of which 7 were waited for; matrix products, arithmetic and copies ran while one was open for 0% of the time, Pallas kernels for 0%

commit v1 on v0

v1 whole, which is shorter than its diff:
```python
import functools

import jax
import jax.numpy as jnp
from jax import lax
from jax.experimental import pallas as pl
from jax.experimental.pallas import tpu as pltpu
from jax.sharding import PartitionSpec as P

MESH = pl.DeviceIdType.MESH
F32 = jnp.float32
BF16 = jnp.bfloat16

BLOCK = 64
LANES = 128
STREAMS = 2
CHUNKS = 8


def halves(x):
    hi = x.astype(BF16)
    return hi, (x - hi.astype(F32)).astype(BF16)


def picked(x, table):
    hi, lo = halves(x)
    return jnp.dot(hi, table, preferred_element_type=F32) + jnp.dot(lo, table, preferred_element_type=F32)


def placed(table, x):
    hi, lo = halves(x)
    dims = (((1,), (1,)), ((), ()))
    return lax.dot_general(table, hi, dims, preferred_element_type=F32) + lax.dot_general(
        table, lo, dims, preferred_element_type=F32
    )


def column_sums(parts):
    at = lax.broadcasted_iota(jnp.int32, parts[0].shape, 0)
    low = at < 4
    four = [
        jnp.where(low, parts[s], parts[s + 4]) + pltpu.roll(jnp.where(low, parts[s + 4], parts[s]), 4, 0)
        for s in range(4)
    ]
    low = (at & 2) == 0
    two = [
        jnp.where(low, four[s], pltpu.roll(four[s + 2], 2, 0)) + jnp.where(low, pltpu.roll(four[s], 6, 0), four[s + 2])
        for s in range(2)
    ]
    low = (at & 1) == 0
    return jnp.where(low, two[0], pltpu.roll(two[1], 1, 0)) + jnp.where(low, pltpu.roll(two[0], 7, 0), two[1])


def total(terms):
    while len(terms) > 1:
        terms = [terms[i] + terms[i + 1] if i + 1 < len(terms) else terms[i] for i in range(0, len(terms), 2)]
    return terms[0]


def act(mats, vecs, outs, count, width):
    def tile(t, _):
        lanes = pl.ds(pl.multiple_of(t * LANES, LANES), LANES)
        x = [[vecs[pl.ds(r * BLOCK + 8 * g, 8), lanes] for g in range(8)] for r in range(count)]

        def group(q, _):
            parts = [[] for _ in range(count)]
            for a in range(8):
                first = pl.multiple_of(q * (8 * BLOCK) + a * BLOCK, BLOCK)
                m = [mats[pl.ds(first + 8 * g, 8), lanes] for g in range(8)]
                for r in range(count):
                    parts[r].append(total([m[g] * x[r][g] for g in range(8)]))
            for r in range(count):
                outs[pl.ds(pl.multiple_of(r * BLOCK + 8 * q, 8), 8), lanes] = column_sums(parts[r])
            return 0

        return lax.fori_loop(0, 8, group, 0)

    lax.fori_loop(0, width // LANES, tile, 0)


def act_back(mats, vecs, outs, count, width):
    def tile(t, _):
        lanes = pl.ds(pl.multiple_of(t * LANES, LANES), LANES)

        def group(q, sums):
            sums = list(sums)
            v = [vecs[pl.ds(pl.multiple_of(r * BLOCK + 8 * q, 8), 8), lanes] for r in range(count)]
            for a in range(8):
                first = pl.multiple_of(q * (8 * BLOCK) + a * BLOCK, BLOCK)
                z = [jnp.broadcast_to(v[r][a : a + 1], (8, LANES)) for r in range(count)]
                for g in range(8):
                    m = mats[pl.ds(first + 8 * g, 8), lanes]
                    for r in range(count):
                        sums[r * 8 + g] = sums[r * 8 + g] + m * z[r]
            return tuple(sums)

        zero = jnp.zeros((8, LANES), F32)
        sums = lax.fori_loop(0, 8, group, (zero,) * (8 * count))
        for r in range(count):
            for g in range(8):
                outs[pl.ds(r * BLOCK + 8 * g, 8), lanes] = sums[r * 8 + g]
        return 0

    lax.fori_loop(0, width // LANES, tile, 0)


def stood_up(v):
    n = v.shape[0]
    both = jnp.concatenate([v, pltpu.roll(v, BLOCK, 1), jnp.zeros((LANES - 2 * n, LANES), F32)], axis=0)
    return both.T[:BLOCK]


def laid_down(v, n):
    flat = jnp.concatenate([v, v], axis=0).T
    lane = lax.broadcasted_iota(jnp.int32, (n, LANES), 1)
    return jnp.where(lane < BLOCK, flat[:n], flat[n : 2 * n])


def kernel(
    nrow, ncol, rhs, mats, rows, cols, diag, couple, out,
    raw, mt, ohc, ohr, ohf, dt, ct, fields, xt, work, done, small, small_out, term, rs, ag, face, fx, wide, fin, cbuf,
    raw_sem, row_send, row_recv, rs_send, rs_recv, ag_send, ag_recv, fx_send, fx_recv, fin_send, fin_recv, c_send, c_recv,
):
    nbf = rhs.shape[0]
    nz = rows.shape[1]
    d, r, c = lax.axis_index("depth"), lax.axis_index("row"), lax.axis_index("col")

    def at_row(i):
        return lax.rem(r + i, nrow)

    def at_col(i):
        return lax.rem(c + i, ncol)

    def send(src, dst, send_sem, recv_sem, where):
        pltpu.make_async_remote_copy(
            src_ref=src, dst_ref=dst, send_sem=send_sem, recv_sem=recv_sem, device_id=where, device_id_type=MESH
        ).start()

    def await_bytes(ref, sem):
        pltpu.make_async_copy(ref, ref, sem).wait()

    def each(low, high, body):
        def step(i, _):
            body(i)
            return 0

        lax.fori_loop(low, high, step, 0)

    barrier = pltpu.get_barrier_semaphore()

    def greet(where):
        pl.semaphore_signal(barrier, inc=1, device_id=where, device_id_type=MESH)

    each(1, ncol, lambda i: greet((d, r, at_col(i))))
    each(1, nrow, lambda i: greet((d, at_row(i), c)))
    each(0, nrow, lambda i: greet((1 - d, at_row(i), c)))

    width = mats.shape[1] // CHUNKS
    pieces = [
        pltpu.make_async_copy(mats.at[:, pl.ds(i * width, width)], raw.at[:, pl.ds(i * width, width)], raw_sem.at[i])
        for i in range(CHUNKS)
    ]
    for piece in pieces:
        piece.start()

    pl.semaphore_wait(barrier, (ncol - 1) + (2 * nrow - 1))

    for s in range(STREAMS):
        part = pl.ds(s * LANES, LANES)
        fields[s, 0] = rhs[:, part]
        each(
            1, nrow,
            lambda i: send(rhs.at[:, part], fields.at[s, i], row_send.at[s], row_recv.at[s], (d, at_row(i), c)),
        )

    @pl.when(d == 1)
    def _():
        cbuf[pl.ds(r, 1)] = couple[...][None]
        each(1, nrow, lambda i: send(couple, cbuf.at[r], c_send, c_recv, (1, at_row(i), c)))
        each(0, nrow, lambda i: send(couple, cbuf.at[r], c_send, c_recv, (0, at_row(i), c)))

    brow, bcol = rows[...], cols[...]
    turned_row = (((c - (brow >> 5)) & (ncol - 1)) << 5) | (brow & 31)
    turned_col = (((r - (bcol >> 5)) & (nrow - 1)) << 5) | (bcol & 31)

    def table(position, count):
        return (lax.broadcasted_iota(jnp.int32, (count, nz), 0) == position).astype(BF16)

    ohr[...] = table(turned_row, ncol * nbf)
    ohc[...] = table(turned_col, nrow * nbf)
    at_face = (bcol & 31) == jnp.where(d == 0, nbf - 1, 0)
    ohf[...] = table(jnp.where(at_face, bcol >> 5, -1), LANES)

    def turn_diag(j):
        lanes = pl.ds(pl.multiple_of(j * LANES, LANES), LANES)
        two = diag[:, lanes]
        dt[lanes, :] = jnp.concatenate([two, two, jnp.zeros((LANES - 2 * nbf, LANES), F32)], axis=0).T

    each(0, diag.shape[1] // LANES, turn_diag)

    for i, piece in enumerate(pieces):
        piece.wait()

        def turn(j):
            lanes = pl.ds(pl.multiple_of(i * width + j * LANES, LANES), LANES)
            for t in range(nz // LANES):
                ks = pl.ds(t * LANES, LANES)
                mt[lanes, ks] = raw[ks, lanes].T

        each(0, width // LANES, turn)

    for s in range(STREAMS):
        await_bytes(fields.at[s, pl.ds(0, nrow - 1)], row_recv.at[s])
        xt[s] = picked(fields[s].reshape(nrow * nbf, LANES).T, ohc[...])

    def turn_couple():
        def one(j):
            two = cbuf[:, pl.ds(j, 1), :].reshape(nrow, LANES)
            full = jnp.concatenate([two, two, jnp.zeros((LANES - 2 * nrow, LANES), F32)], axis=0)
            ct[pl.ds(pl.multiple_of(j * LANES, LANES), LANES), :] = full.T

        each(0, ct.shape[0] // LANES, one)

    def forward(use, s, vecs):
        act(mt, vecs, done, 2, nz)
        term[use, s] = placed(ohr[...], done[...]).reshape(ncol, nbf, LANES)
        each(
            1, ncol,
            lambda i: send(
                term.at[use, s, i], rs.at[use, s, i - 1], rs_send.at[use, s], rs_recv.at[use, s],
                (d, r, at_col(ncol - i)),
            ),
        )

    def middle(use, s, field):
        await_bytes(rs.at[use, s], rs_recv.at[use, s])
        small[...] = stood_up(field + term[use, s, 0] + total([rs[use, s, i] for i in range(ncol - 1)]))
        act(dt, small, small_out, 1, LANES)
        ag[use, s, 0] = laid_down(small_out[...], nbf)
        each(
            1, ncol,
            lambda i: send(
                ag.at[use, s, 0], ag.at[use, s, i], ag_send.at[use, s], ag_recv.at[use, s], (d, r, at_col(i))
            ),
        )

    def backward(use, s):
        await_bytes(ag.at[use, s, pl.ds(0, ncol - 1)], ag_recv.at[use, s])
        work[...] = picked(ag[use, s].reshape(ncol * nbf, LANES).T, ohr[...])
        act_back(mt, work, done, 2, nz)

    def face_out(use, s, own):
        here = lax.broadcasted_iota(jnp.int32, (nrow, LANES), 0) == r
        face[s] = placed(ohf[...], done[...])[:nrow] + jnp.where(here, ag[use, s, 0, own : own + 1], 0.0)
        each(
            0, nrow,
            lambda i: send(face.at[s], fx.at[s, i], fx_send.at[s], fx_recv.at[s], (1 - d, at_row(i), c)),
        )

    def face_in(s, own, action):
        await_bytes(fx.at[s], fx_recv.at[s])
        small[...] = stood_up(total([fx[s, i] for i in range(nrow)]))
        action(ct, small, small_out, 1, LANES)
        moved = small_out[...]
        taken = jnp.concatenate([moved, pltpu.roll(moved, LANES - nrow, 1)], axis=0)
        work[...] = xt[s] - picked(taken, ohf[...])
        here = lax.broadcasted_iota(jnp.int32, (nrow, LANES), 0) == r
        mine = jnp.sum(jnp.where(here, laid_down(moved, nrow), 0.0), axis=0, keepdims=True)
        at_own = lax.broadcasted_iota(jnp.int32, (nbf, LANES), 0) == own
        return fields[s, 0] - jnp.where(at_own, mine, 0.0)

    def widen(s):
        wide[s] = placed(ohc[...], done[...]).reshape(nrow, nbf, LANES)
        each(
            1, nrow,
            lambda i: send(
                wide.at[s, i], fin.at[s, i - 1], fin_send.at[s], fin_recv.at[s], (d, at_row(nrow - i), c)
            ),
        )

    def finish(use, s):
        await_bytes(fin.at[s], fin_recv.at[s])
        out[:, pl.ds(s * LANES, LANES)] = ag[use, s, 0] + wide[s, 0] + total([fin[s, i] for i in range(nrow - 1)])

    every = range(STREAMS)

    @pl.when(d == 0)
    def _():
        for s in every:
            forward(0, s, xt.at[s])
        for s in every:
            middle(0, s, fields[s, 0])
        for s in every:
            backward(0, s)
            face_out(0, s, nbf - 1)
        await_bytes(cbuf, c_recv)
        turn_couple()
        held = []
        for s in every:
            held.append(face_in(s, nbf - 1, act_back))
            forward(1, s, work)
        for s in every:
            middle(1, s, held[s])
        for s in every:
            backward(1, s)
            widen(s)
        for s in every:
            finish(1, s)
        for s in every:
            await_bytes(term.at[1, s, pl.ds(0, ncol - 1)], rs_send.at[1, s])
            await_bytes(ag.at[1, s, pl.ds(0, ncol - 1)], ag_send.at[1, s])

    @pl.when(d == 1)
    def _():
        await_bytes(cbuf.at[pl.ds(0, nrow - 1)], c_recv)
        turn_couple()
        held = []
        for s in every:
            held.append(face_in(s, 0, act))
            forward(0, s, work)
        for s in every:
            middle(0, s, held[s])
        for s in every:
            backward(0, s)
            face_out(0, s, 0)
            widen(s)
        for s in every:
            finish(0, s)
        await_bytes(cbuf.at[pl.ds(0, nrow - 1)], c_send)
        await_bytes(cbuf, c_send)

    for s in every:
        await_bytes(fields.at[s, pl.ds(0, nrow - 1)], row_send.at[s])
        await_bytes(term.at[0, s, pl.ds(0, ncol - 1)], rs_send.at[0, s])
        await_bytes(ag.at[0, s, pl.ds(0, ncol - 1)], ag_send.at[0, s])
        await_bytes(fx.at[s], fx_send.at[s])
        await_bytes(wide.at[s, pl.ds(0, nrow - 1)], fin_send.at[s])


def per_device(nrow, ncol, rhs, factor_blocks, block_rows, block_cols, diag_inverse, coupling):
    nbf = rhs.shape[1]
    nz, size = factor_blocks.shape[-2:]
    vm = pl.BlockSpec(memory_space=pltpu.VMEM)
    dma = pltpu.SemaphoreType.DMA
    got = pl.pallas_call(
        functools.partial(kernel, nrow, ncol),
        out_shape=jax.ShapeDtypeStruct((nbf, rhs.shape[2]), F32),
        in_specs=[vm, pl.BlockSpec(memory_space=pl.ANY), vm, vm, vm, vm],
        out_specs=vm,
        scratch_shapes=[
            pltpu.VMEM((nz, size), F32),
            pltpu.VMEM((size, nz), F32),
            pltpu.VMEM((nrow * nbf, nz), BF16),
            pltpu.VMEM((ncol * nbf, nz), BF16),
            pltpu.VMEM((LANES, nz), BF16),
            pltpu.VMEM((size, LANES), F32),
            pltpu.VMEM((size, LANES), F32),
            pltpu.VMEM((STREAMS, nrow, nbf, LANES), F32),
            pltpu.VMEM((STREAMS, LANES, nz), F32),
            pltpu.VMEM((LANES, nz), F32),
            pltpu.VMEM((LANES, nz), F32),
            pltpu.VMEM((BLOCK, LANES), F32),
            pltpu.VMEM((BLOCK, LANES), F32),
            pltpu.VMEM((2, STREAMS, ncol, nbf, LANES), F32),
            pltpu.VMEM((2, STREAMS, ncol - 1, nbf, LANES), F32),
            pltpu.VMEM((2, STREAMS, ncol, nbf, LANES), F32),
            pltpu.VMEM((STREAMS, nrow, LANES), F32),
            pltpu.VMEM((STREAMS, nrow, nrow, LANES), F32),
            pltpu.VMEM((STREAMS, nrow, nbf, LANES), F32),
            pltpu.VMEM((STREAMS, nrow - 1, nbf, LANES), F32),
            pltpu.VMEM((nrow, size // LANES, LANES), F32),
            dma((CHUNKS,)),
            dma((STREAMS,)), dma((STREAMS,)),
            dma((2, STREAMS)), dma((2, STREAMS)),
            dma((2, STREAMS)), dma((2, STREAMS)),
            dma((STREAMS,)), dma((STREAMS,)),
            dma((STREAMS,)), dma((STREAMS,)),
            dma, dma,
        ],
        compiler_params=pltpu.CompilerParams(
            collective_id=0, has_side_effects=True, vmem_limit_bytes=56 * 1024 * 1024
        ),
    )(
        rhs[0],
        factor_blocks.reshape(nz, size),
        block_rows.reshape(1, nz),
        block_cols.reshape(1, nz),
        diag_inverse[0],
        coupling.reshape(size // LANES, LANES),
    )
    return got[None]


def solution(mesh):
    placed_as = (
        P("depth", ("row", "col"), None),
        P("depth", "row", "col", None, None),
        P("depth", "row", "col", None),
        P("depth", "row", "col", None),
        P("depth", ("row", "col"), None),
        P("depth", ("row", "col"), None),
    )
    return jax.shard_map(
        functools.partial(per_device, mesh.shape["row"], mesh.shape["col"]),
        mesh=mesh,
        in_specs=placed_as,
        out_specs=P("depth", ("row", "col"), None),
        check_vma=False,
    )
```

time: 731 us -> 105 us (0.14); the launches traced: 721 us -> 105 us
  waiting for transfers between devices: 336 us -> 0 us
  blocking collectives: 148 us -> 0 us
  matrix products: 144 us -> 0 us
  Pallas kernels: 0 us -> 104 us
  local copies, waits for them, and re-layouts: 44.2 us -> 1.38 us
  other arithmetic: 30.6 us -> 0 us
  between operations: 14.3 us -> 0.01 us
    reduce_scatter x6 -> x0, waiting for transfers between devices: 335 us -> none  [the longest x3 230 us: solve(): lax.psum_scatter(term, 'col', scatter_dimension=0, tiled=True) + field]
    all_gather x6 -> x0, blocking collectives: 148 us -> none  [the longest x3 78 us: solve(): columns = lax.all_gather(field, 'row', axis=0, tiled=True)]
    dot_general x11 -> x0, matrix products: 144 us -> none  [the longest x7 92.2 us: mix(): jnp.einsum('kab,krb->kra', mats, shaped, precision=lax.Precision.HIGHEST)]
    pallas_call x0 -> x1, Pallas kernels: none -> 104 us  [per_device(): pl.pallas_call(functools.partial(kernel, nrow, ncol), out_shape=jax.Shape...]
    scatter-add x6 -> x0, other arithmetic: 24.1 us -> none  [the longest x3 12.2 us: solve(): jax.ops.segment_sum(mix(mats, columns[sources]), targets, num_segments=nc...]
    another operation x5 -> x0, local copies, waits for them, and re-layouts: 16.9 us -> none  [the longest x1 16.3 us: per_device(): mats = factor_blocks[0, 0, 0].reshape(NZ, BLOCK, BLOCK)]
    gather x12 -> x0, local copies, waits for them, and re-layouts: 10.6 us -> none  [the longest x6 5.29 us: solve(): columns[sources]]
    unnamed x10 -> x1, local copies, waits for them, and re-layouts: 9.78 us -> 1.38 us
  transfers between devices with their start and end apart: 8 -> 0, of which waited for: 7 -> 0; matrix products, arithmetic and copies ran while one was open for 0% -> 0% of each run, Pallas kernels for 0% -> 0%
where the time goes in v1:
time: 105 us
  Pallas kernels  104 us (99%)
  local copies, waits for them, and re-layouts  1.38 us (1%)
    pallas_call x1, Pallas kernels, per_device(): pl.pallas_call(functools.partial(kernel, nrow, ncol), out_shape=jax.Shape...  104 us

profile of v1, /device:TPU:32, one launch (start us, length us, event | category | flops | bytes accessed | tf_op | source)
XLA Modules:
  0.0 105.1 jit_solution(15023911724250415557)
XLA Ops:
  0.0 103.7 %shard_map.64 = f32[32,256]{1,0:T(8,128)} custom-call(f32[32,256]{1,0:T(8,128)} %bitcast.10, f32[512,4096]{1,0:T(8,128)} %bitcast.7, s32[1,512]{1,0:T(1,128)} %bitcast.12, s32[1,512]{1,0:T(1,128)} %bitcast.13, f32[32,4096]{1,0:T(8,128)} %bitcast.8, f32[32,128]{1,0:T(8,128)} %bitcast.11), custom_call_target="tpu_custom_call" | custom-call | tf_op jit(solution)/shard_map/pallas_call | solution.py:345
  103.7 1.4 %copy.8 = f32[1,32,256]{2,1,0:T(8,128)} copy(f32[1,32,256]{2,1,0:T(8,128)} %bitcast.9) | data formatting | bytes 65536

commit v2 on v1

--- a/solution.py
+++ b/solution.py
@@ -14,7 +14,7 @@
 BLOCK = 64
 LANES = 128
 STREAMS = 2
-CHUNKS = 8
+TURNED = 4
 
 
 def halves(x):
@@ -57,39 +57,36 @@
     return terms[0]
 
 
-def act(mats, vecs, outs, count, width):
+def act(mats, vecs, outs, count):
     def tile(t, _):
-        lanes = pl.ds(pl.multiple_of(t * LANES, LANES), LANES)
-        x = [[vecs[pl.ds(r * BLOCK + 8 * g, 8), lanes] for g in range(8)] for r in range(count)]
+        x = [[vecs[t, pl.ds(r * BLOCK + 8 * g, 8), :] for g in range(8)] for r in range(count)]
 
         def group(q, _):
             parts = [[] for _ in range(count)]
             for a in range(8):
                 first = pl.multiple_of(q * (8 * BLOCK) + a * BLOCK, BLOCK)
-                m = [mats[pl.ds(first + 8 * g, 8), lanes] for g in range(8)]
+                m = [mats[t, pl.ds(first + 8 * g, 8), :] for g in range(8)]
                 for r in range(count):
                     parts[r].append(total([m[g] * x[r][g] for g in range(8)]))
             for r in range(count):
-                outs[pl.ds(pl.multiple_of(r * BLOCK + 8 * q, 8), 8), lanes] = column_sums(parts[r])
+                outs[t, pl.ds(pl.multiple_of(r * BLOCK + 8 * q, 8), 8), :] = column_sums(parts[r])
             return 0
 
         return lax.fori_loop(0, 8, group, 0)
 
-    lax.fori_loop(0, width // LANES, tile, 0)
-
-
-def act_back(mats, vecs, outs, count, width):
+    lax.fori_loop(0, mats.shape[0], tile, 0)
+
+
+def act_back(mats, vecs, outs, count):
     def tile(t, _):
-        lanes = pl.ds(pl.multiple_of(t * LANES, LANES), LANES)
-
         def group(q, sums):
             sums = list(sums)
-            v = [vecs[pl.ds(pl.multiple_of(r * BLOCK + 8 * q, 8), 8), lanes] for r in range(count)]
+            v = [vecs[t, pl.ds(pl.multiple_of(r * BLOCK + 8 * q, 8), 8), :] for r in range(count)]
             for a in range(8):
                 first = pl.multiple_of(q * (8 * BLOCK) + a * BLOCK, BLOCK)
                 z = [jnp.broadcast_to(v[r][a : a + 1], (8, LANES)) for r in range(count)]
                 for g in range(8):
-                    m = mats[pl.ds(first + 8 * g, 8), lanes]
+                    m = mats[t, pl.ds(first + 8 * g, 8), :]
                     for r in range(count):
                         sums[r * 8 + g] = sums[r * 8 + g] + m * z[r]
             return tuple(sums)
@@ -98,10 +95,18 @@
         sums = lax.fori_loop(0, 8, group, (zero,) * (8 * count))
         for r in range(count):
             for g in range(8):
-                outs[pl.ds(r * BLOCK + 8 * g, 8), lanes] = sums[r * 8 + g]
+                outs[t, pl.ds(r * BLOCK + 8 * g, 8), :] = sums[r * 8 + g]
         return 0
 
-    lax.fori_loop(0, width // LANES, tile, 0)
+    lax.fori_loop(0, mats.shape[0], tile, 0)
+
+
+def tiles(x):
+    return [x[:, LANES * t : LANES * (t + 1)] for t in range(x.shape[1] // LANES)]
+
+
+def joined(ref):
+    return jnp.concatenate([ref[t] for t in range(ref.shape[0])], axis=1)
 
 
 def stood_up(v):
@@ -155,13 +160,13 @@
     each(1, nrow, lambda i: greet((d, at_row(i), c)))
     each(0, nrow, lambda i: greet((1 - d, at_row(i), c)))
 
-    width = mats.shape[1] // CHUNKS
-    pieces = [
-        pltpu.make_async_copy(mats.at[:, pl.ds(i * width, width)], raw.at[:, pl.ds(i * width, width)], raw_sem.at[i])
-        for i in range(CHUNKS)
-    ]
-    for piece in pieces:
-        piece.start()
+    pieces = raw.shape[0]
+
+    def piece(j):
+        lanes = pl.ds(pl.multiple_of(j * LANES, LANES), LANES)
+        return pltpu.make_async_copy(mats.at[:, lanes], raw.at[j], raw_sem.at[j])
+
+    each(0, pieces, lambda j: piece(j).start())
 
     pl.semaphore_wait(barrier, (ncol - 1) + (2 * nrow - 1))
 
@@ -191,39 +196,46 @@
     at_face = (bcol & 31) == jnp.where(d == 0, nbf - 1, 0)
     ohf[...] = table(jnp.where(at_face, bcol >> 5, -1), LANES)
 
-    def turn_diag(j):
-        lanes = pl.ds(pl.multiple_of(j * LANES, LANES), LANES)
-        two = diag[:, lanes]
-        dt[lanes, :] = jnp.concatenate([two, two, jnp.zeros((LANES - 2 * nbf, LANES), F32)], axis=0).T
-
-    each(0, diag.shape[1] // LANES, turn_diag)
-
-    for i, piece in enumerate(pieces):
-        piece.wait()
-
-        def turn(j):
-            lanes = pl.ds(pl.multiple_of(i * width + j * LANES, LANES), LANES)
+    def turn(i):
+        group = [i * TURNED + u for u in range(TURNED)]
+        for j in group:
+            piece(j).wait()
+        for j in group:
             for t in range(nz // LANES):
-                ks = pl.ds(t * LANES, LANES)
-                mt[lanes, ks] = raw[ks, lanes].T
-
-        each(0, width // LANES, turn)
+                mt[t, pl.ds(pl.multiple_of(j * LANES, LANES), LANES), :] = raw[j, pl.ds(t * LANES, LANES), :].T
+
+    each(0, pieces // TURNED, turn)
+
+    def fill(ref, x):
+        for t, part in enumerate(tiles(x)):
+            ref[t] = part
 
     for s in range(STREAMS):
         await_bytes(fields.at[s, pl.ds(0, nrow - 1)], row_recv.at[s])
-        xt[s] = picked(fields[s].reshape(nrow * nbf, LANES).T, ohc[...])
+        fill(xt.at[s], picked(fields[s].reshape(nrow * nbf, LANES).T, ohc[...]))
+
+    def turn_diag():
+        def some(i):
+            for u in range(TURNED):
+                lanes = pl.ds(pl.multiple_of((i * TURNED + u) * LANES, LANES), LANES)
+                two = diag[:, lanes]
+                dt[0, lanes, :] = jnp.concatenate([two, two, jnp.zeros((LANES - 2 * nbf, LANES), F32)], axis=0).T
+
+        each(0, dt.shape[1] // (TURNED * LANES), some)
 
     def turn_couple():
-        def one(j):
-            two = cbuf[:, pl.ds(j, 1), :].reshape(nrow, LANES)
-            full = jnp.concatenate([two, two, jnp.zeros((LANES - 2 * nrow, LANES), F32)], axis=0)
-            ct[pl.ds(pl.multiple_of(j * LANES, LANES), LANES), :] = full.T
-
-        each(0, ct.shape[0] // LANES, one)
+        def some(i):
+            for u in range(TURNED):
+                j = i * TURNED + u
+                two = cbuf[:, pl.ds(j, 1), :].reshape(nrow, LANES)
+                full = jnp.concatenate([two, two, jnp.zeros((LANES - 2 * nrow, LANES), F32)], axis=0)
+                ct[0, pl.ds(pl.multiple_of(j * LANES, LANES), LANES), :] = full.T
+
+        each(0, ct.shape[1] // (TURNED * LANES), some)
 
     def forward(use, s, vecs):
-        act(mt, vecs, done, 2, nz)
-        term[use, s] = placed(ohr[...], done[...]).reshape(ncol, nbf, LANES)
+        act(mt, vecs, done, 2)
+        term[use, s] = placed(ohr[...], joined(done)).reshape(ncol, nbf, LANES)
         each(
             1, ncol,
             lambda i: send(
@@ -234,9 +246,9 @@
 
     def middle(use, s, field):
         await_bytes(rs.at[use, s], rs_recv.at[use, s])
-        small[...] = stood_up(field + term[use, s, 0] + total([rs[use, s, i] for i in range(ncol - 1)]))
-        act(dt, small, small_out, 1, LANES)
-        ag[use, s, 0] = laid_down(small_out[...], nbf)
+        small[0] = stood_up(field + term[use, s, 0] + total([rs[use, s, i] for i in range(ncol - 1)]))
+        act(dt, small, small_out, 1)
+        ag[use, s, 0] = laid_down(small_out[0], nbf)
         each(
             1, ncol,
             lambda i: send(
@@ -246,12 +258,12 @@
 
     def backward(use, s):
         await_bytes(ag.at[use, s, pl.ds(0, ncol - 1)], ag_recv.at[use, s])
-        work[...] = picked(ag[use, s].reshape(ncol * nbf, LANES).T, ohr[...])
-        act_back(mt, work, done, 2, nz)
+        fill(work, picked(ag[use, s].reshape(ncol * nbf, LANES).T, ohr[...]))
+        act_back(mt, work, done, 2)
 
     def face_out(use, s, own):
         here = lax.broadcasted_iota(jnp.int32, (nrow, LANES), 0) == r
-        face[s] = placed(ohf[...], done[...])[:nrow] + jnp.where(here, ag[use, s, 0, own : own + 1], 0.0)
+        face[s] = placed(ohf[...], joined(done))[:nrow] + jnp.where(here, ag[use, s, 0, own : own + 1], 0.0)
         each(
             0, nrow,
             lambda i: send(face.at[s], fx.at[s, i], fx_send.at[s], fx_recv.at[s], (1 - d, at_row(i), c)),
@@ -259,18 +271,19 @@
 
     def face_in(s, own, action):
         await_bytes(fx.at[s], fx_recv.at[s])
-        small[...] = stood_up(total([fx[s, i] for i in range(nrow)]))
-        action(ct, small, small_out, 1, LANES)
-        moved = small_out[...]
+        small[0] = stood_up(total([fx[s, i] for i in range(nrow)]))
+        action(ct, small, small_out, 1)
+        moved = small_out[0]
         taken = jnp.concatenate([moved, pltpu.roll(moved, LANES - nrow, 1)], axis=0)
-        work[...] = xt[s] - picked(taken, ohf[...])
+        for t, part in enumerate(tiles(picked(taken, ohf[...]))):
+            work[t] = xt[s, t] - part
         here = lax.broadcasted_iota(jnp.int32, (nrow, LANES), 0) == r
         mine = jnp.sum(jnp.where(here, laid_down(moved, nrow), 0.0), axis=0, keepdims=True)
         at_own = lax.broadcasted_iota(jnp.int32, (nbf, LANES), 0) == own
         return fields[s, 0] - jnp.where(at_own, mine, 0.0)
 
     def widen(s):
-        wide[s] = placed(ohc[...], done[...]).reshape(nrow, nbf, LANES)
+        wide[s] = placed(ohc[...], joined(done)).reshape(nrow, nbf, LANES)
         each(
             1, nrow,
             lambda i: send(
@@ -288,6 +301,7 @@
     def _():
         for s in every:
             forward(0, s, xt.at[s])
+        turn_diag()
         for s in every:
             middle(0, s, fields[s, 0])
         for s in every:
@@ -314,6 +328,7 @@
     def _():
         await_bytes(cbuf.at[pl.ds(0, nrow - 1)], c_recv)
         turn_couple()
+        turn_diag()
         held = []
         for s in every:
             held.append(face_in(s, 0, act))
@@ -348,19 +363,19 @@
         in_specs=[vm, pl.BlockSpec(memory_space=pl.ANY), vm, vm, vm, vm],
         out_specs=vm,
         scratch_shapes=[
-            pltpu.VMEM((nz, size), F32),
-            pltpu.VMEM((size, nz), F32),
+            pltpu.VMEM((size // LANES, nz, LANES), F32),
+            pltpu.VMEM((nz // LANES, size, LANES), F32),
             pltpu.VMEM((nrow * nbf, nz), BF16),
             pltpu.VMEM((ncol * nbf, nz), BF16),
             pltpu.VMEM((LANES, nz), BF16),
-            pltpu.VMEM((size, LANES), F32),
-            pltpu.VMEM((size, LANES), F32),
+            pltpu.VMEM((1, size, LANES), F32),
+            pltpu.VMEM((1, size, LANES), F32),
             pltpu.VMEM((STREAMS, nrow, nbf, LANES), F32),
-            pltpu.VMEM((STREAMS, LANES, nz), F32),
-            pltpu.VMEM((LANES, nz), F32),
-            pltpu.VMEM((LANES, nz), F32),
-            pltpu.VMEM((BLOCK, LANES), F32),
-            pltpu.VMEM((BLOCK, LANES), F32),
+            pltpu.VMEM((STREAMS, nz // LANES, LANES, LANES), F32),
+            pltpu.VMEM((nz // LANES, LANES, LANES), F32),
+            pltpu.VMEM((nz // LANES, LANES, LANES), F32),
+            pltpu.VMEM((1, BLOCK, LANES), F32),
+            pltpu.VMEM((1, BLOCK, LANES), F32),
             pltpu.VMEM((2, STREAMS, ncol, nbf, LANES), F32),
             pltpu.VMEM((2, STREAMS, ncol - 1, nbf, LANES), F32),
             pltpu.VMEM((2, STREAMS, ncol, nbf, LANES), F32),
@@ -369,7 +384,7 @@
             pltpu.VMEM((STREAMS, nrow, nbf, LANES), F32),
             pltpu.VMEM((STREAMS, nrow - 1, nbf, LANES), F32),
             pltpu.VMEM((nrow, size // LANES, LANES), F32),
-            dma((CHUNKS,)),
+            dma((size // LANES,)),
             dma((STREAMS,)), dma((STREAMS,)),
             dma((2, STREAMS)), dma((2, STREAMS)),
             dma((2, STREAMS)), dma((2, STREAMS)),

time: 105 us -> 86.7 us (0.83)
  Pallas kernels: 104 us -> 85 us
    pallas_call x1, Pallas kernels: 104 us -> 85 us  [per_device(): pl.pallas_call(functools.partial(kernel, nrow, ncol), out_shape=jax.Shape...]
where the time goes in v2:
time: 86.7 us; the launch traced here: 86.4 us
  Pallas kernels  85 us (98%)
  local copies, waits for them, and re-layouts  1.38 us (2%)
    pallas_call x1, Pallas kernels, per_device(): pl.pallas_call(functools.partial(kernel, nrow, ncol), out_shape=jax.Shape...  85 us

profile of v2, /device:TPU:32, one launch (start us, length us, event | category | flops | bytes accessed | tf_op | source)
XLA Modules:
  0.0 86.4 jit_solution(2499357974673292533)
XLA Ops:
  0.0 85.0 %shard_map.64 = f32[32,256]{1,0:T(8,128)} custom-call(f32[32,256]{1,0:T(8,128)} %bitcast.10, f32[512,4096]{1,0:T(8,128)} %bitcast.7, s32[1,512]{1,0:T(1,128)} %bitcast.12, s32[1,512]{1,0:T(1,128)} %bitcast.13, f32[32,4096]{1,0:T(8,128)} %bitcast.8, f32[32,128]{1,0:T(8,128)} %bitcast.11), custom_call_target="tpu_custom_call" | custom-call | tf_op jit(solution)/shard_map/pallas_call | solution.py:360
  85.0 1.4 %copy.8 = f32[1,32,256]{2,1,0:T(8,128)} copy(f32[1,32,256]{2,1,0:T(8,128)} %bitcast.9) | data formatting | bytes 65536

commit v3 on v2

--- a/solution.py
+++ b/solution.py
@@ -1,4 +1,5 @@
 import functools
+import math
 
 import jax
 import jax.numpy as jnp
@@ -123,18 +124,33 @@
 
 def kernel(
     nrow, ncol, rhs, mats, rows, cols, diag, couple, out,
-    raw, mt, ohc, ohr, ohf, dt, ct, fields, xt, work, done, small, small_out, term, rs, ag, face, fx, wide, fin, cbuf,
-    raw_sem, row_send, row_recv, rs_send, rs_recv, ag_send, ag_recv, fx_send, fx_recv, fin_send, fin_recv, c_send, c_recv,
+    raw, mt, ohc, ohr, ohf, dt, ct, fields, xt, work, done, small, small_out, term, rs, ag, face, fx, wide, fin, cbuf, diag0,
+    index0, raw_sem, row_send, row_recv, rs_send, rs_recv, ag_send, ag_recv, fx_send, fx_recv, fin_send, fin_recv, c_send,
+    c_recv, early_send, early_recv, late_send, late_recv,
 ):
     nbf = rhs.shape[0]
     nz = rows.shape[1]
+    side = math.isqrt(ncol)
     d, r, c = lax.axis_index("depth"), lax.axis_index("row"), lax.axis_index("col")
+    cy, cx = lax.div(c, side), lax.rem(c, side)
 
     def at_row(i):
         return lax.rem(r + i, nrow)
 
     def at_col(i):
-        return lax.rem(c + i, ncol)
+        return lax.rem(cy + lax.div(i, side), side) * side + lax.rem(cx + lax.rem(i, side), side)
+
+    def back_col(i):
+        return lax.rem(cy - lax.div(i, side) + side, side) * side + lax.rem(cx - lax.rem(i, side) + side, side)
+
+    def far_row(j):
+        return nrow // 2 + lax.div(j + 1, 2) * (1 - 2 * lax.rem(j, 2))
+
+    def far_side(j):
+        return lax.rem(side // 2 + lax.div(j * (j + 1), 2), side)
+
+    def far_col(j):
+        return far_side(lax.div(j, side)) * side + far_side(lax.rem(j, side))
 
     def send(src, dst, send_sem, recv_sem, where):
         pltpu.make_async_remote_copy(
@@ -151,14 +167,21 @@
 
         lax.fori_loop(low, high, step, 0)
 
+    def each_col(body):
+        each(0, ncol - 1, lambda j: body(far_col(j)))
+
+    def each_row(body):
+        each(0, nrow - 1, lambda j: body(far_row(j)))
+
     barrier = pltpu.get_barrier_semaphore()
 
     def greet(where):
         pl.semaphore_signal(barrier, inc=1, device_id=where, device_id_type=MESH)
 
-    each(1, ncol, lambda i: greet((d, r, at_col(i))))
-    each(1, nrow, lambda i: greet((d, at_row(i), c)))
-    each(0, nrow, lambda i: greet((1 - d, at_row(i), c)))
+    each_row(lambda i: greet((d, at_row(i), c)))
+    each_row(lambda i: greet((1 - d, at_row(i), c)))
+    each_col(lambda i: greet((d, r, at_col(i))))
+    greet((1 - d, r, c))
 
     pieces = raw.shape[0]
 
@@ -172,29 +195,34 @@
 
     for s in range(STREAMS):
         part = pl.ds(s * LANES, LANES)
-        fields[s, 0] = rhs[:, part]
-        each(
-            1, nrow,
-            lambda i: send(rhs.at[:, part], fields.at[s, i], row_send.at[s], row_recv.at[s], (d, at_row(i), c)),
-        )
+        fields[0, s, 0] = rhs[:, part]
+        each_row(lambda i: send(rhs.at[:, part], fields.at[0, s, i], row_send.at[s], row_recv.at[s], (d, at_row(i), c)))
+
+    @pl.when(d == 0)
+    def _():
+        index0[0, 0:1] = rows[...]
+        index0[0, 1:2] = cols[...]
+        send(index0.at[0], index0.at[1], early_send.at[0], early_recv.at[0], (1, r, c))
+        send(diag, diag0, early_send.at[1], early_recv.at[1], (1, r, c))
 
     @pl.when(d == 1)
     def _():
         cbuf[pl.ds(r, 1)] = couple[...][None]
-        each(1, nrow, lambda i: send(couple, cbuf.at[r], c_send, c_recv, (1, at_row(i), c)))
-        each(0, nrow, lambda i: send(couple, cbuf.at[r], c_send, c_recv, (0, at_row(i), c)))
-
-    brow, bcol = rows[...], cols[...]
-    turned_row = (((c - (brow >> 5)) & (ncol - 1)) << 5) | (brow & 31)
-    turned_col = (((r - (bcol >> 5)) & (nrow - 1)) << 5) | (bcol & 31)
-
-    def table(position, count):
-        return (lax.broadcasted_iota(jnp.int32, (count, nz), 0) == position).astype(BF16)
-
-    ohr[...] = table(turned_row, ncol * nbf)
-    ohc[...] = table(turned_col, nrow * nbf)
-    at_face = (bcol & 31) == jnp.where(d == 0, nbf - 1, 0)
-    ohf[...] = table(jnp.where(at_face, bcol >> 5, -1), LANES)
+        each_row(lambda i: send(couple, cbuf.at[r], c_send, c_recv, (1, at_row(i), c)))
+
+    def tables(use, brow, bcol, own_face):
+        oy, ox = (brow >> 5) // side, (brow >> 5) % side
+        slot_row = ((cy - oy) & (side - 1)) * side + ((cx - ox) & (side - 1))
+        slot_col = (r - (bcol >> 5)) & (nrow - 1)
+
+        def table(position, count):
+            return (lax.broadcasted_iota(jnp.int32, (count, nz), 0) == position).astype(BF16)
+
+        ohr[use] = table((slot_row << 5) | (brow & 31), ncol * nbf)
+        ohc[use] = table((slot_col << 5) | (bcol & 31), nrow * nbf)
+        ohf[use] = table(jnp.where((bcol & 31) == own_face, bcol >> 5, -1), LANES)
+
+    tables(0, rows[...], cols[...], jnp.where(d == 0, nbf - 1, 0))
 
     def turn(i):
         group = [i * TURNED + u for u in range(TURNED)]
@@ -202,7 +230,7 @@
             piece(j).wait()
         for j in group:
             for t in range(nz // LANES):
-                mt[t, pl.ds(pl.multiple_of(j * LANES, LANES), LANES), :] = raw[j, pl.ds(t * LANES, LANES), :].T
+                mt[0, t, pl.ds(pl.multiple_of(j * LANES, LANES), LANES), :] = raw[j, pl.ds(t * LANES, LANES), :].T
 
     each(0, pieces // TURNED, turn)
 
@@ -211,17 +239,18 @@
             ref[t] = part
 
     for s in range(STREAMS):
-        await_bytes(fields.at[s, pl.ds(0, nrow - 1)], row_recv.at[s])
-        fill(xt.at[s], picked(fields[s].reshape(nrow * nbf, LANES).T, ohc[...]))
-
-    def turn_diag():
+        await_bytes(fields.at[0, s, pl.ds(0, nrow - 1)], row_recv.at[s])
+        fill(xt.at[0, s], picked(fields[0, s].reshape(nrow * nbf, LANES).T, ohc[0]))
+
+    def turn_diag(use, given):
         def some(i):
             for u in range(TURNED):
                 lanes = pl.ds(pl.multiple_of((i * TURNED + u) * LANES, LANES), LANES)
-                two = diag[:, lanes]
-                dt[0, lanes, :] = jnp.concatenate([two, two, jnp.zeros((LANES - 2 * nbf, LANES), F32)], axis=0).T
-
-        each(0, dt.shape[1] // (TURNED * LANES), some)
+                two = given[:, lanes]
+                full = jnp.concatenate([two, two, jnp.zeros((LANES - 2 * nbf, LANES), F32)], axis=0)
+                dt[use, 0, lanes, :] = full.T
+
+        each(0, dt.shape[2] // (TURNED * LANES), some)
 
     def turn_couple():
         def some(i):
@@ -234,122 +263,145 @@
         each(0, ct.shape[1] // (TURNED * LANES), some)
 
     def forward(use, s, vecs):
-        act(mt, vecs, done, 2)
-        term[use, s] = placed(ohr[...], joined(done)).reshape(ncol, nbf, LANES)
-        each(
-            1, ncol,
+        act(mt.at[use], vecs, done.at[s], 2)
+        term[use, s] = placed(ohr[use], joined(done.at[s])).reshape(ncol, nbf, LANES)
+        each_col(
             lambda i: send(
-                term.at[use, s, i], rs.at[use, s, i - 1], rs_send.at[use, s], rs_recv.at[use, s],
-                (d, r, at_col(ncol - i)),
-            ),
+                term.at[use, s, i], rs.at[use, s, i - 1], rs_send.at[use, s], rs_recv.at[use, s], (d, r, back_col(i))
+            )
         )
 
     def middle(use, s, field):
         await_bytes(rs.at[use, s], rs_recv.at[use, s])
         small[0] = stood_up(field + term[use, s, 0] + total([rs[use, s, i] for i in range(ncol - 1)]))
-        act(dt, small, small_out, 1)
+        act(dt.at[use], small, small_out, 1)
         ag[use, s, 0] = laid_down(small_out[0], nbf)
-        each(
-            1, ncol,
+        each_col(
             lambda i: send(
                 ag.at[use, s, 0], ag.at[use, s, i], ag_send.at[use, s], ag_recv.at[use, s], (d, r, at_col(i))
-            ),
+            )
         )
 
     def backward(use, s):
         await_bytes(ag.at[use, s, pl.ds(0, ncol - 1)], ag_recv.at[use, s])
-        fill(work, picked(ag[use, s].reshape(ncol * nbf, LANES).T, ohr[...]))
-        act_back(mt, work, done, 2)
+        fill(work, picked(ag[use, s].reshape(ncol * nbf, LANES).T, ohr[use]))
+        act_back(mt.at[use], work, done.at[s], 2)
 
     def face_out(use, s, own):
         here = lax.broadcasted_iota(jnp.int32, (nrow, LANES), 0) == r
-        face[s] = placed(ohf[...], joined(done))[:nrow] + jnp.where(here, ag[use, s, 0, own : own + 1], 0.0)
-        each(
-            0, nrow,
-            lambda i: send(face.at[s], fx.at[s, i], fx_send.at[s], fx_recv.at[s], (1 - d, at_row(i), c)),
-        )
-
-    def face_in(s, own, action):
-        await_bytes(fx.at[s], fx_recv.at[s])
-        small[0] = stood_up(total([fx[s, i] for i in range(nrow)]))
+        face[s] = placed(ohf[use], joined(done.at[s]))[:nrow] + jnp.where(here, ag[use, s, 0, own : own + 1], 0.0)
+
+    def face_in(use, s, own, action, take):
+        small[0] = stood_up(total([fx[take, s, i] for i in range(nrow)]))
         action(ct, small, small_out, 1)
         moved = small_out[0]
         taken = jnp.concatenate([moved, pltpu.roll(moved, LANES - nrow, 1)], axis=0)
-        for t, part in enumerate(tiles(picked(taken, ohf[...]))):
-            work[t] = xt[s, t] - part
+        for t, part in enumerate(tiles(picked(taken, ohf[use]))):
+            work[t] = xt[use, s, t] - part
         here = lax.broadcasted_iota(jnp.int32, (nrow, LANES), 0) == r
         mine = jnp.sum(jnp.where(here, laid_down(moved, nrow), 0.0), axis=0, keepdims=True)
         at_own = lax.broadcasted_iota(jnp.int32, (nbf, LANES), 0) == own
-        return fields[s, 0] - jnp.where(at_own, mine, 0.0)
-
-    def widen(s):
-        wide[s] = placed(ohc[...], joined(done)).reshape(nrow, nbf, LANES)
-        each(
-            1, nrow,
-            lambda i: send(
-                wide.at[s, i], fin.at[s, i - 1], fin_send.at[s], fin_recv.at[s], (d, at_row(nrow - i), c)
-            ),
-        )
-
-    def finish(use, s):
-        await_bytes(fin.at[s], fin_recv.at[s])
-        out[:, pl.ds(s * LANES, LANES)] = ag[use, s, 0] + wide[s, 0] + total([fin[s, i] for i in range(nrow - 1)])
+        return fields[use, s, 0] - jnp.where(at_own, mine, 0.0)
+
+    def widen(use, s):
+        wide[use, s] = placed(ohc[use], joined(done.at[s])).reshape(nrow, nbf, LANES)
 
     every = range(STREAMS)
 
     @pl.when(d == 0)
     def _():
         for s in every:
-            forward(0, s, xt.at[s])
-        turn_diag()
-        for s in every:
-            middle(0, s, fields[s, 0])
+            forward(0, s, xt.at[0, s])
+        turn_diag(0, diag)
+        for s in every:
+            middle(0, s, fields[0, s, 0])
         for s in every:
             backward(0, s)
             face_out(0, s, nbf - 1)
-        await_bytes(cbuf, c_recv)
-        turn_couple()
-        held = []
-        for s in every:
-            held.append(face_in(s, nbf - 1, act_back))
-            forward(1, s, work)
-        for s in every:
-            middle(1, s, held[s])
-        for s in every:
-            backward(1, s)
-            widen(s)
-        for s in every:
-            finish(1, s)
-        for s in every:
-            await_bytes(term.at[1, s, pl.ds(0, ncol - 1)], rs_send.at[1, s])
-            await_bytes(ag.at[1, s, pl.ds(0, ncol - 1)], ag_send.at[1, s])
+            each_row(lambda i: send(face.at[s], fx.at[0, s, i], fx_send.at[0, s], fx_recv.at[0, s], (1, at_row(i), c)))
+            send(face.at[s], fx.at[0, s, 0], fx_send.at[0, s], fx_recv.at[0, s], (1, r, c))
+        send(xt.at[0], xt.at[1], late_send.at[0], late_recv.at[0], (1, r, c))
+        send(fields.at[0, :, 0], fields.at[1, :, 0], late_send.at[1], late_recv.at[1], (1, r, c))
+        for t in range(nz // LANES):
+            send(mt.at[0, t], mt.at[1, t], late_send.at[2 + t], late_recv.at[2 + t], (1, r, c))
+        for s in every:
+            await_bytes(fin.at[s], fin_recv.at[s])
+            out[:, pl.ds(s * LANES, LANES)] = total([fin[s, i] for i in range(nrow)])
+        for s in every:
+            await_bytes(fx.at[0, s], fx_send.at[0, s])
+        pltpu.make_async_copy(index0.at[0], index0.at[0], early_send.at[0]).wait()
+        await_bytes(diag, early_send.at[1])
+        await_bytes(xt.at[0], late_send.at[0])
+        await_bytes(fields.at[0, :, 0], late_send.at[1])
+        for t in range(nz // LANES):
+            await_bytes(mt.at[0, t], late_send.at[2 + t])
 
     @pl.when(d == 1)
     def _():
         await_bytes(cbuf.at[pl.ds(0, nrow - 1)], c_recv)
         turn_couple()
-        turn_diag()
+        turn_diag(0, diag)
+        await_bytes(index0.at[1], early_recv.at[0])
+        tables(1, index0[1, 0:1], index0[1, 1:2], nbf - 1)
+        await_bytes(diag0, early_recv.at[1])
+        turn_diag(1, diag0)
         held = []
         for s in every:
-            held.append(face_in(s, 0, act))
+            await_bytes(fx.at[0, s], fx_recv.at[0, s])
+            held.append(face_in(0, s, 0, act, 0))
             forward(0, s, work)
         for s in every:
             middle(0, s, held[s])
         for s in every:
             backward(0, s)
             face_out(0, s, 0)
-            widen(s)
-        for s in every:
-            finish(0, s)
+            each_row(lambda i: send(face.at[s], fx.at[1, s, i], fx_send.at[1, s], fx_recv.at[1, s], (1, at_row(i), c)))
+            fx[1, s, 0] = face[s]
+        for s in every:
+            widen(0, s)
+            each_row(
+                lambda i: send(
+                    wide.at[0, s, i], fin.at[s, i], fin_send.at[0, s], fin_recv.at[s], (1, at_row(nrow - i), c)
+                )
+            )
+        await_bytes(xt.at[1], late_recv.at[0])
+        await_bytes(fields.at[1, :, 0], late_recv.at[1])
+        for t in range(nz // LANES):
+            await_bytes(mt.at[1, t], late_recv.at[2 + t])
+        held = []
+        for s in every:
+            await_bytes(fx.at[1, s, pl.ds(0, nrow - 1)], fx_recv.at[1, s])
+            held.append(face_in(1, s, nbf - 1, act_back, 1))
+            forward(1, s, work)
+        for s in every:
+            await_bytes(fin.at[s, pl.ds(0, nrow - 1)], fin_recv.at[s])
+            out[:, pl.ds(s * LANES, LANES)] = (
+                ag[0, s, 0] + wide[0, s, 0] + total([fin[s, i] for i in range(1, nrow)])
+            )
+        for s in every:
+            middle(1, s, held[s])
+        for s in every:
+            backward(1, s)
+            widen(1, s)
+            wide[1, s, 0] += ag[1, s, 0]
+            each_row(
+                lambda i: send(
+                    wide.at[1, s, i], fin.at[s, i], fin_send.at[1, s], fin_recv.at[s], (0, at_row(nrow - i), c)
+                )
+            )
+            send(wide.at[1, s, 0], fin.at[s, 0], fin_send.at[1, s], fin_recv.at[s], (0, r, c))
         await_bytes(cbuf.at[pl.ds(0, nrow - 1)], c_send)
-        await_bytes(cbuf, c_send)
+        for s in every:
+            await_bytes(fx.at[1, s, pl.ds(0, nrow - 1)], fx_send.at[1, s])
+            await_bytes(wide.at[0, s, pl.ds(0, nrow - 1)], fin_send.at[0, s])
+            await_bytes(wide.at[1, s], fin_send.at[1, s])
+            await_bytes(term.at[1, s, pl.ds(0, ncol - 1)], rs_send.at[1, s])
+            await_bytes(ag.at[1, s, pl.ds(0, ncol - 1)], ag_send.at[1, s])
 
     for s in every:
-        await_bytes(fields.at[s, pl.ds(0, nrow - 1)], row_send.at[s])
+        await_bytes(fields.at[0, s, pl.ds(0, nrow - 1)], row_send.at[s])
         await_bytes(term.at[0, s, pl.ds(0, ncol - 1)], rs_send.at[0, s])
         await_bytes(ag.at[0, s, pl.ds(0, ncol - 1)], ag_send.at[0, s])
-        await_bytes(fx.at[s], fx_send.at[s])
-        await_bytes(wide.at[s, pl.ds(0, nrow - 1)], fin_send.at[s])
 
 
 def per_device(nrow, ncol, rhs, factor_blocks, block_rows, block_cols, diag_inverse, coupling):
@@ -364,33 +416,37 @@
         out_specs=vm,
         scratch_shapes=[
             pltpu.VMEM((size // LANES, nz, LANES), F32),
-            pltpu.VMEM((nz // LANES, size, LANES), F32),
-            pltpu.VMEM((nrow * nbf, nz), BF16),
-            pltpu.VMEM((ncol * nbf, nz), BF16),
-            pltpu.VMEM((LANES, nz), BF16),
+            pltpu.VMEM((2, nz // LANES, size, LANES), F32),
+            pltpu.VMEM((2, nrow * nbf, nz), BF16),
+            pltpu.VMEM((2, ncol * nbf, nz), BF16),
+            pltpu.VMEM((2, LANES, nz), BF16),
+            pltpu.VMEM((2, 1, size, LANES), F32),
             pltpu.VMEM((1, size, LANES), F32),
-            pltpu.VMEM((1, size, LANES), F32),
-            pltpu.VMEM((STREAMS, nrow, nbf, LANES), F32),
+            pltpu.VMEM((2, STREAMS, nrow, nbf, LANES), F32),
+            pltpu.VMEM((2, STREAMS, nz // LANES, LANES, LANES), F32),
+            pltpu.VMEM((nz // LANES, LANES, LANES), F32),
             pltpu.VMEM((STREAMS, nz // LANES, LANES, LANES), F32),
-            pltpu.VMEM((nz // LANES, LANES, LANES), F32),
-            pltpu.VMEM((nz // LANES, LANES, LANES), F32),
             pltpu.VMEM((1, BLOCK, LANES), F32),
             pltpu.VMEM((1, BLOCK, LANES), F32),
             pltpu.VMEM((2, STREAMS, ncol, nbf, LANES), F32),
             pltpu.VMEM((2, STREAMS, ncol - 1, nbf, LANES), F32),
             pltpu.VMEM((2, STREAMS, ncol, nbf, LANES), F32),
             pltpu.VMEM((STREAMS, nrow, LANES), F32),
-            pltpu.VMEM((STREAMS, nrow, nrow, LANES), F32),
+            pltpu.VMEM((2, STREAMS, nrow, nrow, LANES), F32),
+            pltpu.VMEM((2, STREAMS, nrow, nbf, LANES), F32),
             pltpu.VMEM((STREAMS, nrow, nbf, LANES), F32),
-            pltpu.VMEM((STREAMS, nrow - 1, nbf, LANES), F32),
             pltpu.VMEM((nrow, size // LANES, LANES), F32),
+            pltpu.VMEM((nbf, size), F32),
+            pltpu.VMEM((2, 2, nz), jnp.int32),
             dma((size // LANES,)),
             dma((STREAMS,)), dma((STREAMS,)),
             dma((2, STREAMS)), dma((2, STREAMS)),
             dma((2, STREAMS)), dma((2, STREAMS)),
-            dma((STREAMS,)), dma((STREAMS,)),
-            dma((STREAMS,)), dma((STREAMS,)),
+            dma((2, STREAMS)), dma((2, STREAMS)),
+            dma((2, STREAMS)), dma((STREAMS,)),
             dma, dma,
+            dma((2,)), dma((2,)),
+            dma((2 + nz // LANES,)), dma((2 + nz // LANES,)),
         ],
         compiler_params=pltpu.CompilerParams(
             collective_id=0, has_side_effects=True, vmem_limit_bytes=56 * 1024 * 1024

time: 86.7 us -> 82.8 us (0.955)
  Pallas kernels: 85 us -> 81.1 us
    pallas_call x1, Pallas kernels: 85 us -> 81.1 us  [per_device(): pl.pallas_call(functools.partial(kernel, nrow, ncol), out_shape=jax.Shape...]
where the time goes in v3:
time: 82.8 us; the launch traced here: 82.5 us
  Pallas kernels  81.1 us (98%)
  local copies, waits for them, and re-layouts  1.38 us (2%)
    pallas_call x1, Pallas kernels, per_device(): pl.pallas_call(functools.partial(kernel, nrow, ncol), out_shape=jax.Shape...  81.1 us

profile of v3, /device:TPU:32, one launch (start us, length us, event | category | flops | bytes accessed | tf_op | source)
XLA Modules:
  0.0 82.5 jit_solution(13434267566935091166)
XLA Ops:
  0.0 81.1 %shard_map.64 = f32[32,256]{1,0:T(8,128)} custom-call(f32[32,256]{1,0:T(8,128)} %bitcast.10, f32[512,4096]{1,0:T(8,128)} %bitcast.7, s32[1,512]{1,0:T(1,128)} %bitcast.12, s32[1,512]{1,0:T(1,128)} %bitcast.13, f32[32,4096]{1,0:T(8,128)} %bitcast.8, f32[32,128]{1,0:T(8,128)} %bitcast.11), custom_call_target="tpu_custom_call" | custom-call | tf_op jit(solution)/shard_map/pallas_call | solution.py:412
  81.1 1.4 %copy.8 = f32[1,32,256]{2,1,0:T(8,128)} copy(f32[1,32,256]{2,1,0:T(8,128)} %bitcast.9) | data formatting | bytes 65536

commit v4 on v3

--- a/solution.py
+++ b/solution.py
@@ -24,16 +24,16 @@
 
 
 def picked(x, table):
-    hi, lo = halves(x)
-    return jnp.dot(hi, table, preferred_element_type=F32) + jnp.dot(lo, table, preferred_element_type=F32)
+    n = x.shape[0]
+    both = jnp.dot(jnp.concatenate(halves(x), axis=0), table, preferred_element_type=F32)
+    return both[:n] + both[n:]
 
 
 def placed(table, x):
-    hi, lo = halves(x)
+    n = x.shape[0]
     dims = (((1,), (1,)), ((), ()))
-    return lax.dot_general(table, hi, dims, preferred_element_type=F32) + lax.dot_general(
-        table, lo, dims, preferred_element_type=F32
-    )
+    both = lax.dot_general(table, jnp.concatenate(halves(x), axis=0), dims, preferred_element_type=F32)
+    return both[:, :n] + both[:, n:]
 
 
 def column_sums(parts):
@@ -73,7 +73,7 @@
                 outs[t, pl.ds(pl.multiple_of(r * BLOCK + 8 * q, 8), 8), :] = column_sums(parts[r])
             return 0
 
-        return lax.fori_loop(0, 8, group, 0)
+        return lax.fori_loop(0, mats.shape[1] // (8 * BLOCK), group, 0)
 
     lax.fori_loop(0, mats.shape[0], tile, 0)
 
@@ -122,11 +122,24 @@
     return jnp.where(lane < BLOCK, flat[:n], flat[n : 2 * n])
 
 
+def stood_up_twice(v):
+    pair = [v, pltpu.roll(v, BLOCK, 1)]
+    return jnp.concatenate(pair + pair, axis=0).T[:BLOCK]
+
+
+def laid_down_halves(v, n):
+    flat = jnp.concatenate([v] * 4, axis=0).T
+    quarter = lax.broadcasted_iota(jnp.int32, (n, LANES), 1) // (BLOCK // 2)
+    low = jnp.where(quarter == 0, flat[:n], flat[2 * n : 3 * n])
+    high = jnp.where(quarter == 2, flat[n : 2 * n], flat[3 * n :])
+    return jnp.where(quarter < 2, low, high)
+
+
 def kernel(
-    nrow, ncol, rhs, mats, rows, cols, diag, couple, out,
-    raw, mt, ohc, ohr, ohf, dt, ct, fields, xt, work, done, small, small_out, term, rs, ag, face, fx, wide, fin, cbuf, diag0,
+    nrow, ncol, rhs_in, mats, rows_in, cols_in, diag_in, couple_in, out,
+    rhs, rows, cols, diag, couple, raw, mt, ohc, ohr, ohf, dt, ct, fields, xt, work, done, small, small_out, term, rs, ag, face, fx, wide, fin, cbuf, diag0,
     index0, raw_sem, row_send, row_recv, rs_send, rs_recv, ag_send, ag_recv, fx_send, fx_recv, fin_send, fin_recv, c_send,
-    c_recv, early_send, early_recv, late_send, late_recv,
+    c_recv, early_send, early_recv, late_send, late_recv, in_sem,
 ):
     nbf = rhs.shape[0]
     nz = rows.shape[1]
@@ -189,26 +202,28 @@
         lanes = pl.ds(pl.multiple_of(j * LANES, LANES), LANES)
         return pltpu.make_async_copy(mats.at[:, lanes], raw.at[j], raw_sem.at[j])
 
+    inputs = [
+        pltpu.make_async_copy(src, dst, in_sem.at[i])
+        for i, (src, dst) in enumerate(
+            ((rhs_in, rhs), (rows_in, rows), (cols_in, cols), (couple_in, couple), (diag_in, diag))
+        )
+    ]
+    for copy in inputs:
+        copy.start()
     each(0, pieces, lambda j: piece(j).start())
-
+    for copy in inputs:
+        copy.wait()
     pl.semaphore_wait(barrier, (ncol - 1) + (2 * nrow - 1))
 
-    for s in range(STREAMS):
+    def share_field(s):
         part = pl.ds(s * LANES, LANES)
         fields[0, s, 0] = rhs[:, part]
         each_row(lambda i: send(rhs.at[:, part], fields.at[0, s, i], row_send.at[s], row_recv.at[s], (d, at_row(i), c)))
 
     @pl.when(d == 0)
     def _():
-        index0[0, 0:1] = rows[...]
-        index0[0, 1:2] = cols[...]
-        send(index0.at[0], index0.at[1], early_send.at[0], early_recv.at[0], (1, r, c))
-        send(diag, diag0, early_send.at[1], early_recv.at[1], (1, r, c))
-
-    @pl.when(d == 1)
-    def _():
-        cbuf[pl.ds(r, 1)] = couple[...][None]
-        each_row(lambda i: send(couple, cbuf.at[r], c_send, c_recv, (1, at_row(i), c)))
+        for s in range(STREAMS):
+            share_field(s)
 
     def tables(use, brow, bcol, own_face):
         oy, ox = (brow >> 5) // side, (brow >> 5) % side
@@ -234,6 +249,13 @@
 
     each(0, pieces // TURNED, turn)
 
+    @pl.when(d == 1)
+    def _():
+        for s in range(STREAMS):
+            share_field(s)
+        cbuf[pl.ds(r, 1)] = couple[...][None]
+        each_row(lambda i: send(couple, cbuf.at[r], c_send, c_recv, (1, at_row(i), c)))
+
     def fill(ref, x):
         for t, part in enumerate(tiles(x)):
             ref[t] = part
@@ -243,14 +265,16 @@
         fill(xt.at[0, s], picked(fields[0, s].reshape(nrow * nbf, LANES).T, ohc[0]))
 
     def turn_diag(use, given):
+        apart = given.shape[1] // (2 * LANES)
+
         def some(i):
             for u in range(TURNED):
-                lanes = pl.ds(pl.multiple_of((i * TURNED + u) * LANES, LANES), LANES)
-                two = given[:, lanes]
-                full = jnp.concatenate([two, two, jnp.zeros((LANES - 2 * nbf, LANES), F32)], axis=0)
-                dt[use, 0, lanes, :] = full.T
-
-        each(0, dt.shape[2] // (TURNED * LANES), some)
+                j = i * TURNED + u
+                low, high = (given[:, pl.ds(pl.multiple_of(k * LANES, LANES), LANES)] for k in (j, j + apart))
+                full = jnp.concatenate([low, low, high, high], axis=0)
+                dt[use, 0, pl.ds(pl.multiple_of(j * LANES, LANES), LANES), :] = full.T
+
+        each(0, apart // TURNED, some)
 
     def turn_couple():
         def some(i):
@@ -273,9 +297,9 @@
 
     def middle(use, s, field):
         await_bytes(rs.at[use, s], rs_recv.at[use, s])
-        small[0] = stood_up(field + term[use, s, 0] + total([rs[use, s, i] for i in range(ncol - 1)]))
+        small[0] = stood_up_twice(field + term[use, s, 0] + total([rs[use, s, i] for i in range(ncol - 1)]))
         act(dt.at[use], small, small_out, 1)
-        ag[use, s, 0] = laid_down(small_out[0], nbf)
+        ag[use, s, 0] = laid_down_halves(small_out[0, : BLOCK // 2], nbf)
         each_col(
             lambda i: send(
                 ag.at[use, s, 0], ag.at[use, s, i], ag_send.at[use, s], ag_recv.at[use, s], (d, r, at_col(i))
@@ -312,6 +336,10 @@
     def _():
         for s in every:
             forward(0, s, xt.at[0, s])
+        index0[0, 0:1] = rows[...]
+        index0[0, 1:2] = cols[...]
+        send(index0.at[0], index0.at[1], early_send.at[0], early_recv.at[0], (1, r, c))
+        send(diag, diag0, early_send.at[1], early_recv.at[1], (1, r, c))
         turn_diag(0, diag)
         for s in every:
             middle(0, s, fields[0, s, 0])
@@ -412,15 +440,20 @@
     got = pl.pallas_call(
         functools.partial(kernel, nrow, ncol),
         out_shape=jax.ShapeDtypeStruct((nbf, rhs.shape[2]), F32),
-        in_specs=[vm, pl.BlockSpec(memory_space=pl.ANY), vm, vm, vm, vm],
+        in_specs=[pl.BlockSpec(memory_space=pl.ANY)] * 6,
         out_specs=vm,
         scratch_shapes=[
+            pltpu.VMEM((nbf, rhs.shape[2]), F32),
+            pltpu.VMEM((1, nz), jnp.int32),
+            pltpu.VMEM((1, nz), jnp.int32),
+            pltpu.VMEM((nbf, size), F32),
+            pltpu.VMEM((size // LANES, LANES), F32),
             pltpu.VMEM((size // LANES, nz, LANES), F32),
             pltpu.VMEM((2, nz // LANES, size, LANES), F32),
             pltpu.VMEM((2, nrow * nbf, nz), BF16),
             pltpu.VMEM((2, ncol * nbf, nz), BF16),
             pltpu.VMEM((2, LANES, nz), BF16),
-            pltpu.VMEM((2, 1, size, LANES), F32),
+            pltpu.VMEM((2, 1, size // 2, LANES), F32),
             pltpu.VMEM((1, size, LANES), F32),
             pltpu.VMEM((2, STREAMS, nrow, nbf, LANES), F32),
             pltpu.VMEM((2, STREAMS, nz // LANES, LANES, LANES), F32),
@@ -447,6 +480,7 @@
             dma, dma,
             dma((2,)), dma((2,)),
             dma((2 + nz // LANES,)), dma((2 + nz // LANES,)),
+            dma((5,)),
         ],
         compiler_params=pltpu.CompilerParams(
             collective_id=0, has_side_effects=True, vmem_limit_bytes=56 * 1024 * 1024

time: 82.8 us -> 78.2 us (0.944)
  Pallas kernels: 81.1 us -> 76.6 us
    pallas_call x1, Pallas kernels: 81.1 us -> 76.6 us  [per_device(): pl.pallas_call(functools.partial(kernel, nrow, ncol), out_shape=jax.Shape...]
where the time goes in v4:
time: 78.2 us; the launch traced here: 78 us
  Pallas kernels  76.6 us (98%)
  local copies, waits for them, and re-layouts  1.38 us (2%)
    pallas_call x1, Pallas kernels, per_device(): pl.pallas_call(functools.partial(kernel, nrow, ncol), out_shape=jax.Shape...  76.6 us

profile of v4, /device:TPU:32, one launch (start us, length us, event | category | flops | bytes accessed | tf_op | source)
XLA Modules:
  0.0 78.0 jit_solution(4040325990376520520)
XLA Ops:
  0.0 76.6 %shard_map.64 = f32[32,256]{1,0:T(8,128)} custom-call(f32[32,256]{1,0:T(8,128)} %bitcast.10, f32[512,4096]{1,0:T(8,128)} %bitcast.7, s32[1,512]{1,0:T(1,128)} %bitcast.12, s32[1,512]{1,0:T(1,128)} %bitcast.13, f32[32,4096]{1,0:T(8,128)} %bitcast.8, f32[32,128]{1,0:T(8,128)} %bitcast.11), custom_call_target="tpu_custom_call" | custom-call | tf_op jit(solution)/shard_map/pallas_call | solution.py:440
  76.7 1.4 %copy.8 = f32[1,32,256]{2,1,0:T(8,128)} copy(f32[1,32,256]{2,1,0:T(8,128)} %bitcast.9) | data formatting | bytes 65536

commit v5 on v4

--- a/solution.py
+++ b/solution.py
@@ -193,8 +193,13 @@
 
     each_row(lambda i: greet((d, at_row(i), c)))
     each_row(lambda i: greet((1 - d, at_row(i), c)))
-    each_col(lambda i: greet((d, r, at_col(i))))
+    each_col(lambda i: greet((1 - d, r, at_col(i))))
     greet((1 - d, r, c))
+
+    @pl.when(d == 1)
+    def _():
+        each_col(lambda i: greet((1, r, at_col(i))))
+
 
     pieces = raw.shape[0]
 
@@ -213,7 +218,7 @@
     each(0, pieces, lambda j: piece(j).start())
     for copy in inputs:
         copy.wait()
-    pl.semaphore_wait(barrier, (ncol - 1) + (2 * nrow - 1))
+    pl.semaphore_wait(barrier, 2 * (nrow - 1) + ncol + (ncol - 1) * d)
 
     def share_field(s):
         part = pl.ds(s * LANES, LANES)
@@ -249,18 +254,11 @@
 
     each(0, pieces // TURNED, turn)
 
-    @pl.when(d == 1)
-    def _():
-        for s in range(STREAMS):
-            share_field(s)
-        cbuf[pl.ds(r, 1)] = couple[...][None]
-        each_row(lambda i: send(couple, cbuf.at[r], c_send, c_recv, (1, at_row(i), c)))
-
     def fill(ref, x):
         for t, part in enumerate(tiles(x)):
             ref[t] = part
 
-    for s in range(STREAMS):
+    def gather_field(s):
         await_bytes(fields.at[0, s, pl.ds(0, nrow - 1)], row_recv.at[s])
         fill(xt.at[0, s], picked(fields[0, s].reshape(nrow * nbf, LANES).T, ohc[0]))
 
@@ -286,105 +284,122 @@
 
         each(0, ct.shape[1] // (TURNED * LANES), some)
 
-    def forward(use, s, vecs):
-        act(mt.at[use], vecs, done.at[s], 2)
-        term[use, s] = placed(ohr[use], joined(done.at[s])).reshape(ncol, nbf, LANES)
+    def forward(p, u, s, vecs):
+        act(mt.at[p], vecs, done.at[s], 2)
+        term[u, s] = placed(ohr[p], joined(done.at[s])).reshape(ncol, nbf, LANES)
         each_col(
+            lambda i: send(term.at[u, s, i], rs.at[u, s, i], rs_send.at[u, s], rs_recv.at[u, s], (1, r, back_col(i)))
+        )
+
+    def middle(p, u, s, summed):
+        small[0] = stood_up_twice(summed)
+        act(dt.at[p], small, small_out, 1)
+        ag[u, s, 0] = laid_down_halves(small_out[0, : BLOCK // 2], nbf)
+        each_col(
+            lambda i: send(ag.at[u, s, 0], ag.at[u, s, i], ag_send.at[u, s], ag_recv.at[u, s], (1, r, at_col(i)))
+        )
+
+    def own_sum(u, s, field):
+        await_bytes(rs.at[u, s, pl.ds(0, ncol - 1)], rs_recv.at[u, s])
+        return field + term[u, s, 0] + total([rs[u, s, i] for i in range(1, ncol)])
+
+    def backward(p, u, s):
+        await_bytes(ag.at[u, s, pl.ds(0, ncol - 1)], ag_recv.at[u, s])
+        fill(work, picked(ag[u, s].reshape(ncol * nbf, LANES).T, ohr[p]))
+        act_back(mt.at[p], work, done.at[s], 2)
+
+    def face_out(p, u, s, own, take):
+        here = lax.broadcasted_iota(jnp.int32, (nrow, LANES), 0) == r
+        face[take, s] = placed(ohf[p], joined(done.at[s]))[:nrow] + jnp.where(here, ag[u, s, 0, own : own + 1], 0.0)
+        each_row(
             lambda i: send(
-                term.at[use, s, i], rs.at[use, s, i - 1], rs_send.at[use, s], rs_recv.at[use, s], (d, r, back_col(i))
+                face.at[take, s], fx.at[take, s, i], fx_send.at[take, s], fx_recv.at[take, s], (1, at_row(i), c)
             )
         )
-
-    def middle(use, s, field):
-        await_bytes(rs.at[use, s], rs_recv.at[use, s])
-        small[0] = stood_up_twice(field + term[use, s, 0] + total([rs[use, s, i] for i in range(ncol - 1)]))
-        act(dt.at[use], small, small_out, 1)
-        ag[use, s, 0] = laid_down_halves(small_out[0, : BLOCK // 2], nbf)
-        each_col(
-            lambda i: send(
-                ag.at[use, s, 0], ag.at[use, s, i], ag_send.at[use, s], ag_recv.at[use, s], (d, r, at_col(i))
-            )
-        )
-
-    def backward(use, s):
-        await_bytes(ag.at[use, s, pl.ds(0, ncol - 1)], ag_recv.at[use, s])
-        fill(work, picked(ag[use, s].reshape(ncol * nbf, LANES).T, ohr[use]))
-        act_back(mt.at[use], work, done.at[s], 2)
-
-    def face_out(use, s, own):
-        here = lax.broadcasted_iota(jnp.int32, (nrow, LANES), 0) == r
-        face[s] = placed(ohf[use], joined(done.at[s]))[:nrow] + jnp.where(here, ag[use, s, 0, own : own + 1], 0.0)
-
-    def face_in(use, s, own, action, take):
+        fx[take, s, 0] = face[take, s]
+
+    def face_in(p, s, own, action, take):
+        await_bytes(fx.at[take, s, pl.ds(0, nrow - 1)], fx_recv.at[take, s])
         small[0] = stood_up(total([fx[take, s, i] for i in range(nrow)]))
         action(ct, small, small_out, 1)
         moved = small_out[0]
         taken = jnp.concatenate([moved, pltpu.roll(moved, LANES - nrow, 1)], axis=0)
-        for t, part in enumerate(tiles(picked(taken, ohf[use]))):
-            work[t] = xt[use, s, t] - part
+        for t, part in enumerate(tiles(picked(taken, ohf[p]))):
+            work[t] = xt[p, s, t] - part
         here = lax.broadcasted_iota(jnp.int32, (nrow, LANES), 0) == r
         mine = jnp.sum(jnp.where(here, laid_down(moved, nrow), 0.0), axis=0, keepdims=True)
         at_own = lax.broadcasted_iota(jnp.int32, (nbf, LANES), 0) == own
-        return fields[use, s, 0] - jnp.where(at_own, mine, 0.0)
-
-    def widen(use, s):
-        wide[use, s] = placed(ohc[use], joined(done.at[s])).reshape(nrow, nbf, LANES)
+        return fields[p, s, 0] - jnp.where(at_own, mine, 0.0)
+
+    def widen(p, s):
+        wide[p, s] = placed(ohc[p], joined(done.at[s])).reshape(nrow, nbf, LANES)
 
     every = range(STREAMS)
+    factor = range(nz // LANES)
 
     @pl.when(d == 0)
     def _():
-        for s in every:
-            forward(0, s, xt.at[0, s])
+        for t in factor[0:2]:
+            send(mt.at[0, t], mt.at[1, t], late_send.at[2 + t], late_recv.at[2 + t], (1, r, c))
+        gather_field(0)
         index0[0, 0:1] = rows[...]
         index0[0, 1:2] = cols[...]
         send(index0.at[0], index0.at[1], early_send.at[0], early_recv.at[0], (1, r, c))
         send(diag, diag0, early_send.at[1], early_recv.at[1], (1, r, c))
-        turn_diag(0, diag)
-        for s in every:
-            middle(0, s, fields[0, s, 0])
-        for s in every:
-            backward(0, s)
-            face_out(0, s, nbf - 1)
-            each_row(lambda i: send(face.at[s], fx.at[0, s, i], fx_send.at[0, s], fx_recv.at[0, s], (1, at_row(i), c)))
-            send(face.at[s], fx.at[0, s, 0], fx_send.at[0, s], fx_recv.at[0, s], (1, r, c))
+        send(fields.at[0, :, 0], fields.at[1, :, 0], late_send.at[1], late_recv.at[1], (1, r, c))
+        for s in every:
+            if s > 0:
+                gather_field(s)
+            forward(0, 2, s, xt.at[0, s])
+            send(term.at[2, s, 0], rs.at[2, s, 0], rs_send.at[2, s], rs_recv.at[2, s], (1, r, c))
+        for t in factor[2:4]:
+            send(mt.at[0, t], mt.at[1, t], late_send.at[2 + t], late_recv.at[2 + t], (1, r, c))
         send(xt.at[0], xt.at[1], late_send.at[0], late_recv.at[0], (1, r, c))
-        send(fields.at[0, :, 0], fields.at[1, :, 0], late_send.at[1], late_recv.at[1], (1, r, c))
-        for t in range(nz // LANES):
-            send(mt.at[0, t], mt.at[1, t], late_send.at[2 + t], late_recv.at[2 + t], (1, r, c))
         for s in every:
             await_bytes(fin.at[s], fin_recv.at[s])
             out[:, pl.ds(s * LANES, LANES)] = total([fin[s, i] for i in range(nrow)])
-        for s in every:
-            await_bytes(fx.at[0, s], fx_send.at[0, s])
         pltpu.make_async_copy(index0.at[0], index0.at[0], early_send.at[0]).wait()
         await_bytes(diag, early_send.at[1])
         await_bytes(xt.at[0], late_send.at[0])
         await_bytes(fields.at[0, :, 0], late_send.at[1])
-        for t in range(nz // LANES):
+        for t in factor:
             await_bytes(mt.at[0, t], late_send.at[2 + t])
+        for s in every:
+            await_bytes(term.at[2, s], rs_send.at[2, s])
 
     @pl.when(d == 1)
     def _():
-        await_bytes(cbuf.at[pl.ds(0, nrow - 1)], c_recv)
-        turn_couple()
-        turn_diag(0, diag)
         await_bytes(index0.at[1], early_recv.at[0])
+        for s in every:
+            share_field(s)
+        cbuf[pl.ds(r, 1)] = couple[...][None]
+        each_row(lambda i: send(couple, cbuf.at[r], c_send, c_recv, (1, at_row(i), c)))
         tables(1, index0[1, 0:1], index0[1, 1:2], nbf - 1)
         await_bytes(diag0, early_recv.at[1])
         turn_diag(1, diag0)
+        await_bytes(fields.at[1, :, 0], late_recv.at[1])
+        for s in every:
+            await_bytes(rs.at[2, s], rs_recv.at[2, s])
+            middle(1, 2, s, fields[1, s, 0] + total([rs[2, s, i] for i in range(ncol)]))
+        turn_diag(0, diag)
+        for s in every:
+            gather_field(s)
+        await_bytes(cbuf.at[pl.ds(0, nrow - 1)], c_recv)
+        turn_couple()
+        for t in factor:
+            await_bytes(mt.at[1, t], late_recv.at[2 + t])
+        for s in every:
+            backward(1, 2, s)
+            face_out(1, 2, s, nbf - 1, 0)
         held = []
         for s in every:
-            await_bytes(fx.at[0, s], fx_recv.at[0, s])
             held.append(face_in(0, s, 0, act, 0))
-            forward(0, s, work)
-        for s in every:
-            middle(0, s, held[s])
-        for s in every:
-            backward(0, s)
-            face_out(0, s, 0)
-            each_row(lambda i: send(face.at[s], fx.at[1, s, i], fx_send.at[1, s], fx_recv.at[1, s], (1, at_row(i), c)))
-            fx[1, s, 0] = face[s]
+            forward(0, 0, s, work)
+        for s in every:
+            middle(0, 0, s, own_sum(0, s, held[s]))
+        for s in every:
+            backward(0, 0, s)
+            face_out(0, 0, s, 0, 1)
         for s in every:
             widen(0, s)
             each_row(
@@ -393,23 +408,19 @@
                 )
             )
         await_bytes(xt.at[1], late_recv.at[0])
-        await_bytes(fields.at[1, :, 0], late_recv.at[1])
-        for t in range(nz // LANES):
-            await_bytes(mt.at[1, t], late_recv.at[2 + t])
         held = []
         for s in every:
-            await_bytes(fx.at[1, s, pl.ds(0, nrow - 1)], fx_recv.at[1, s])
             held.append(face_in(1, s, nbf - 1, act_back, 1))
-            forward(1, s, work)
+            forward(1, 1, s, work)
         for s in every:
             await_bytes(fin.at[s, pl.ds(0, nrow - 1)], fin_recv.at[s])
             out[:, pl.ds(s * LANES, LANES)] = (
                 ag[0, s, 0] + wide[0, s, 0] + total([fin[s, i] for i in range(1, nrow)])
             )
         for s in every:
-            middle(1, s, held[s])
-        for s in every:
-            backward(1, s)
+            middle(1, 1, s, own_sum(1, s, held[s]))
+        for s in every:
+            backward(1, 1, s)
             widen(1, s)
             wide[1, s, 0] += ag[1, s, 0]
             each_row(
@@ -420,16 +431,16 @@
             send(wide.at[1, s, 0], fin.at[s, 0], fin_send.at[1, s], fin_recv.at[s], (0, r, c))
         await_bytes(cbuf.at[pl.ds(0, nrow - 1)], c_send)
         for s in every:
-            await_bytes(fx.at[1, s, pl.ds(0, nrow - 1)], fx_send.at[1, s])
             await_bytes(wide.at[0, s, pl.ds(0, nrow - 1)], fin_send.at[0, s])
             await_bytes(wide.at[1, s], fin_send.at[1, s])
-            await_bytes(term.at[1, s, pl.ds(0, ncol - 1)], rs_send.at[1, s])
-            await_bytes(ag.at[1, s, pl.ds(0, ncol - 1)], ag_send.at[1, s])
+            for take in range(2):
+                await_bytes(fx.at[take, s, pl.ds(0, nrow - 1)], fx_send.at[take, s])
+                await_bytes(term.at[take, s, pl.ds(0, ncol - 1)], rs_send.at[take, s])
+            for u in range(3):
+                await_bytes(ag.at[u, s, pl.ds(0, ncol - 1)], ag_send.at[u, s])
 
     for s in every:
         await_bytes(fields.at[0, s, pl.ds(0, nrow - 1)], row_send.at[s])
-        await_bytes(term.at[0, s, pl.ds(0, ncol - 1)], rs_send.at[0, s])
-        await_bytes(ag.at[0, s, pl.ds(0, ncol - 1)], ag_send.at[0, s])
 
 
 def per_device(nrow, ncol, rhs, factor_blocks, block_rows, block_cols, diag_inverse, coupling):
@@ -461,10 +472,10 @@
             pltpu.VMEM((STREAMS, nz // LANES, LANES, LANES), F32),
             pltpu.VMEM((1, BLOCK, LANES), F32),
             pltpu.VMEM((1, BLOCK, LANES), F32),
-            pltpu.VMEM((2, STREAMS, ncol, nbf, LANES), F32),
-            pltpu.VMEM((2, STREAMS, ncol - 1, nbf, LANES), F32),
-            pltpu.VMEM((2, STREAMS, ncol, nbf, LANES), F32),
-            pltpu.VMEM((STREAMS, nrow, LANES), F32),
+            pltpu.VMEM((3, STREAMS, ncol, nbf, LANES), F32),
+            pltpu.VMEM((3, STREAMS, ncol, nbf, LANES), F32),
+            pltpu.VMEM((3, STREAMS, ncol, nbf, LANES), F32),
+            pltpu.VMEM((2, STREAMS, nrow, LANES), F32),
             pltpu.VMEM((2, STREAMS, nrow, nrow, LANES), F32),
             pltpu.VMEM((2, STREAMS, nrow, nbf, LANES), F32),
             pltpu.VMEM((STREAMS, nrow, nbf, LANES), F32),
@@ -473,8 +484,8 @@
             pltpu.VMEM((2, 2, nz), jnp.int32),
             dma((size // LANES,)),
             dma((STREAMS,)), dma((STREAMS,)),
-            dma((2, STREAMS)), dma((2, STREAMS)),
-            dma((2, STREAMS)), dma((2, STREAMS)),
+            dma((3, STREAMS)), dma((3, STREAMS)),
+            dma((3, STREAMS)), dma((3, STREAMS)),
             dma((2, STREAMS)), dma((2, STREAMS)),
             dma((2, STREAMS)), dma((STREAMS,)),
             dma, dma,

time: 78.2 us -> 75.3 us (0.963)
  Pallas kernels: 76.6 us -> 73.8 us
    pallas_call x1, Pallas kernels: 76.6 us -> 73.8 us  [per_device(): pl.pallas_call(functools.partial(kernel, nrow, ncol), out_shape=jax.Shape...]
where the time goes in v5:
time: 75.3 us; the launch traced here: 75.2 us
  Pallas kernels  73.8 us (98%)
  local copies, waits for them, and re-layouts  1.38 us (2%)
    pallas_call x1, Pallas kernels, per_device(): pl.pallas_call(functools.partial(kernel, nrow, ncol), out_shape=jax.Shape...  73.8 us

profile of v5, /device:TPU:32, one launch (start us, length us, event | category | flops | bytes accessed | tf_op | source)
XLA Modules:
  0.0 75.2 jit_solution(4991348194389513037)
XLA Ops:
  0.0 73.8 %shard_map.64 = f32[32,256]{1,0:T(8,128)} custom-call(f32[32,256]{1,0:T(8,128)} %bitcast.10, f32[512,4096]{1,0:T(8,128)} %bitcast.7, s32[1,512]{1,0:T(1,128)} %bitcast.12, s32[1,512]{1,0:T(1,128)} %bitcast.13, f32[32,4096]{1,0:T(8,128)} %bitcast.8, f32[32,128]{1,0:T(8,128)} %bitcast.11), custom_call_target="tpu_custom_call" | custom-call | tf_op jit(solution)/shard_map/pallas_call | solution.py:451
  73.8 1.4 %copy.8 = f32[1,32,256]{2,1,0:T(8,128)} copy(f32[1,32,256]{2,1,0:T(8,128)} %bitcast.9) | data formatting | bytes 65536

commit v6 on v5

--- a/solution.py
+++ b/solution.py
@@ -36,41 +36,25 @@
     return both[:, :n] + both[:, n:]
 
 
-def column_sums(parts):
-    at = lax.broadcasted_iota(jnp.int32, parts[0].shape, 0)
-    low = at < 4
-    four = [
-        jnp.where(low, parts[s], parts[s + 4]) + pltpu.roll(jnp.where(low, parts[s + 4], parts[s]), 4, 0)
-        for s in range(4)
-    ]
-    low = (at & 2) == 0
-    two = [
-        jnp.where(low, four[s], pltpu.roll(four[s + 2], 2, 0)) + jnp.where(low, pltpu.roll(four[s], 6, 0), four[s + 2])
-        for s in range(2)
-    ]
-    low = (at & 1) == 0
-    return jnp.where(low, two[0], pltpu.roll(two[1], 1, 0)) + jnp.where(low, pltpu.roll(two[0], 7, 0), two[1])
-
-
 def total(terms):
     while len(terms) > 1:
         terms = [terms[i] + terms[i + 1] if i + 1 < len(terms) else terms[i] for i in range(0, len(terms), 2)]
     return terms[0]
 
 
-def act(mats, vecs, outs, count):
+def act(mats, vecs, outs, count, parts):
     def tile(t, _):
         x = [[vecs[t, pl.ds(r * BLOCK + 8 * g, 8), :] for g in range(8)] for r in range(count)]
 
         def group(q, _):
-            parts = [[] for _ in range(count)]
             for a in range(8):
                 first = pl.multiple_of(q * (8 * BLOCK) + a * BLOCK, BLOCK)
                 m = [mats[t, pl.ds(first + 8 * g, 8), :] for g in range(8)]
                 for r in range(count):
-                    parts[r].append(total([m[g] * x[r][g] for g in range(8)]))
+                    parts[r, pl.ds(8 * a, 8), :] = total([m[g] * x[r][g] for g in range(8)])
             for r in range(count):
-                outs[t, pl.ds(pl.multiple_of(r * BLOCK + 8 * q, 8), 8), :] = column_sums(parts[r])
+                rows = total([parts[r, pl.ds(i, 8, stride=8), :] for i in range(8)])
+                outs[t, pl.ds(pl.multiple_of(r * BLOCK + 8 * q, 8), 8), :] = rows
             return 0
 
         return lax.fori_loop(0, mats.shape[1] // (8 * BLOCK), group, 0)
@@ -93,7 +77,7 @@
             return tuple(sums)
 
         zero = jnp.zeros((8, LANES), F32)
-        sums = lax.fori_loop(0, 8, group, (zero,) * (8 * count))
+        sums = lax.fori_loop(0, mats.shape[1] // (8 * BLOCK), group, (zero,) * (8 * count))
         for r in range(count):
             for g in range(8):
                 outs[t, pl.ds(r * BLOCK + 8 * g, 8), :] = sums[r * 8 + g]
@@ -112,8 +96,27 @@
 
 def stood_up(v):
     n = v.shape[0]
-    both = jnp.concatenate([v, pltpu.roll(v, BLOCK, 1), jnp.zeros((LANES - 2 * n, LANES), F32)], axis=0)
-    return both.T[:BLOCK]
+    eighths = [v, pltpu.roll(v, BLOCK, 1)] * 8
+    if 16 * n < LANES:
+        eighths.append(jnp.zeros((LANES - 16 * n, LANES), F32))
+    return jnp.concatenate(eighths, axis=0).T[:BLOCK]
+
+
+def couple_on(ct, small, small_out, parts, x, n):
+    small[0] = x
+    act(ct, small, small_out, 1, parts)
+    o = small_out[0, :8]
+    return jnp.concatenate([o] + [pltpu.roll(o, LANES - 2 * n * i, 1) for i in range(1, 8)], axis=0)
+
+
+def couple_back(ct, small, small_out, parts, z, n):
+    eighth = lax.broadcasted_iota(jnp.int32, (8, LANES), 1) // (2 * n)
+    small[0, :8] = total([jnp.where(eighth == i, z[8 * i : 8 * i + 8], 0.0) for i in range(8)])
+    act_back(ct, small, small_out, 1)
+    o = small_out[0]
+    for i in (4, 2, 1):
+        o = o + pltpu.roll(o, LANES - 2 * n * i, 1)
+    return o
 
 
 def laid_down(v, n):
@@ -137,7 +140,7 @@
 
 def kernel(
     nrow, ncol, rhs_in, mats, rows_in, cols_in, diag_in, couple_in, out,
-    rhs, rows, cols, diag, couple, raw, mt, ohc, ohr, ohf, dt, ct, fields, xt, work, done, small, small_out, term, rs, ag, face, fx, wide, fin, cbuf, diag0,
+    rhs, rows, cols, diag, couple, raw, mt, ohc, ohr, ohf, dt, ct, fields, xt, work, done, small, small_out, parts, term, rs, ag, face, fx, wide, fin, cbuf, diag0,
     index0, raw_sem, row_send, row_recv, rs_send, rs_recv, ag_send, ag_recv, fx_send, fx_recv, fin_send, fin_recv, c_send,
     c_recv, early_send, early_recv, late_send, late_recv, in_sem,
 ):
@@ -151,19 +154,15 @@
         return lax.rem(r + i, nrow)
 
     def at_col(i):
-        return lax.rem(cy + lax.div(i, side), side) * side + lax.rem(cx + lax.rem(i, side), side)
+        return lax.rem(cy + i // side, side) * side + lax.rem(cx + i % side, side)
 
     def back_col(i):
-        return lax.rem(cy - lax.div(i, side) + side, side) * side + lax.rem(cx - lax.rem(i, side) + side, side)
-
-    def far_row(j):
-        return nrow // 2 + lax.div(j + 1, 2) * (1 - 2 * lax.rem(j, 2))
-
-    def far_side(j):
-        return lax.rem(side // 2 + lax.div(j * (j + 1), 2), side)
-
-    def far_col(j):
-        return far_side(lax.div(j, side)) * side + far_side(lax.rem(j, side))
+        return lax.rem(cy - i // side + side, side) * side + lax.rem(cx - i % side + side, side)
+
+    rows_away = sorted(range(1, nrow), key=lambda i: -min(i, nrow - i))
+    cols_away = sorted(
+        range(1, ncol), key=lambda i: -min(i // side, side - i // side) - min(i % side, side - i % side)
+    )
 
     def send(src, dst, send_sem, recv_sem, where):
         pltpu.make_async_remote_copy(
@@ -181,10 +180,12 @@
         lax.fori_loop(low, high, step, 0)
 
     def each_col(body):
-        each(0, ncol - 1, lambda j: body(far_col(j)))
+        for i in cols_away:
+            body(i)
 
     def each_row(body):
-        each(0, nrow - 1, lambda j: body(far_row(j)))
+        for i in rows_away:
+            body(i)
 
     barrier = pltpu.get_barrier_semaphore()
 
@@ -275,17 +276,18 @@
         each(0, apart // TURNED, some)
 
     def turn_couple():
-        def some(i):
-            for u in range(TURNED):
-                j = i * TURNED + u
-                two = cbuf[:, pl.ds(j, 1), :].reshape(nrow, LANES)
-                full = jnp.concatenate([two, two, jnp.zeros((LANES - 2 * nrow, LANES), F32)], axis=0)
-                ct[0, pl.ds(pl.multiple_of(j * LANES, LANES), LANES), :] = full.T
-
-        each(0, ct.shape[1] // (TURNED * LANES), some)
+        apart = ct.shape[1] // LANES
+        for j in range(apart):
+            lots = []
+            for i in range(8):
+                two = cbuf[:, pl.ds(i * apart + j, 1), :].reshape(nrow, LANES)
+                lots += [two, two]
+            if 16 * nrow < LANES:
+                lots.append(jnp.zeros((LANES - 16 * nrow, LANES), F32))
+            ct[0, pl.ds(j * LANES, LANES), :] = jnp.concatenate(lots, axis=0).T
 
     def forward(p, u, s, vecs):
-        act(mt.at[p], vecs, done.at[s], 2)
+        act(mt.at[p], vecs, done.at[s], 2, parts)
         term[u, s] = placed(ohr[p], joined(done.at[s])).reshape(ncol, nbf, LANES)
         each_col(
             lambda i: send(term.at[u, s, i], rs.at[u, s, i], rs_send.at[u, s], rs_recv.at[u, s], (1, r, back_col(i)))
@@ -293,7 +295,7 @@
 
     def middle(p, u, s, summed):
         small[0] = stood_up_twice(summed)
-        act(dt.at[p], small, small_out, 1)
+        act(dt.at[p], small, small_out, 1, parts)
         ag[u, s, 0] = laid_down_halves(small_out[0, : BLOCK // 2], nbf)
         each_col(
             lambda i: send(ag.at[u, s, 0], ag.at[u, s, i], ag_send.at[u, s], ag_recv.at[u, s], (1, r, at_col(i)))
@@ -310,7 +312,7 @@
 
     def face_out(p, u, s, own, take):
         here = lax.broadcasted_iota(jnp.int32, (nrow, LANES), 0) == r
-        face[take, s] = placed(ohf[p], joined(done.at[s]))[:nrow] + jnp.where(here, ag[u, s, 0, own : own + 1], 0.0)
+        face[take, s] = placed(ohf[p, :16], joined(done.at[s]))[:nrow] + jnp.where(here, ag[u, s, 0, own : own + 1], 0.0)
         each_row(
             lambda i: send(
                 face.at[take, s], fx.at[take, s, i], fx_send.at[take, s], fx_recv.at[take, s], (1, at_row(i), c)
@@ -320,9 +322,7 @@
 
     def face_in(p, s, own, action, take):
         await_bytes(fx.at[take, s, pl.ds(0, nrow - 1)], fx_recv.at[take, s])
-        small[0] = stood_up(total([fx[take, s, i] for i in range(nrow)]))
-        action(ct, small, small_out, 1)
-        moved = small_out[0]
+        moved = action(ct, small, small_out, parts, stood_up(total([fx[take, s, i] for i in range(nrow)])), nrow)
         taken = jnp.concatenate([moved, pltpu.roll(moved, LANES - nrow, 1)], axis=0)
         for t, part in enumerate(tiles(picked(taken, ohf[p]))):
             work[t] = xt[p, s, t] - part
@@ -393,7 +393,7 @@
             face_out(1, 2, s, nbf - 1, 0)
         held = []
         for s in every:
-            held.append(face_in(0, s, 0, act, 0))
+            held.append(face_in(0, s, 0, couple_on, 0))
             forward(0, 0, s, work)
         for s in every:
             middle(0, 0, s, own_sum(0, s, held[s]))
@@ -410,7 +410,7 @@
         await_bytes(xt.at[1], late_recv.at[0])
         held = []
         for s in every:
-            held.append(face_in(1, s, nbf - 1, act_back, 1))
+            held.append(face_in(1, s, nbf - 1, couple_back, 1))
             forward(1, 1, s, work)
         for s in every:
             await_bytes(fin.at[s, pl.ds(0, nrow - 1)], fin_recv.at[s])
@@ -465,13 +465,14 @@
             pltpu.VMEM((2, ncol * nbf, nz), BF16),
             pltpu.VMEM((2, LANES, nz), BF16),
             pltpu.VMEM((2, 1, size // 2, LANES), F32),
-            pltpu.VMEM((1, size, LANES), F32),
+            pltpu.VMEM((1, size // 8, LANES), F32),
             pltpu.VMEM((2, STREAMS, nrow, nbf, LANES), F32),
             pltpu.VMEM((2, STREAMS, nz // LANES, LANES, LANES), F32),
             pltpu.VMEM((nz // LANES, LANES, LANES), F32),
             pltpu.VMEM((STREAMS, nz // LANES, LANES, LANES), F32),
             pltpu.VMEM((1, BLOCK, LANES), F32),
             pltpu.VMEM((1, BLOCK, LANES), F32),
+            pltpu.VMEM((2, BLOCK, LANES), F32),
             pltpu.VMEM((3, STREAMS, ncol, nbf, LANES), F32),
             pltpu.VMEM((3, STREAMS, ncol, nbf, LANES), F32),
             pltpu.VMEM((3, STREAMS, ncol, nbf, LANES), F32),

time: 75.3 us -> 72.8 us (0.967)
  Pallas kernels: 73.8 us -> 71 us
    pallas_call x1, Pallas kernels: 73.8 us -> 71 us  [per_device(): pl.pallas_call(functools.partial(kernel, nrow, ncol), out_shape=jax.Shape...]
where the time goes in v6:
time: 72.8 us; the launch traced here: 72.4 us
  Pallas kernels  71 us (98%)
  local copies, waits for them, and re-layouts  1.38 us (2%)
    pallas_call x1, Pallas kernels, per_device(): pl.pallas_call(functools.partial(kernel, nrow, ncol), out_shape=jax.Shape...  71 us

profile of v6, /device:TPU:32, one launch (start us, length us, event | category | flops | bytes accessed | tf_op | source)
XLA Modules:
  0.0 72.4 jit_solution(2680211819478886897)
XLA Ops:
  0.0 71.0 %shard_map.64 = f32[32,256]{1,0:T(8,128)} custom-call(f32[32,256]{1,0:T(8,128)} %bitcast.10, f32[512,4096]{1,0:T(8,128)} %bitcast.7, s32[1,512]{1,0:T(1,128)} %bitcast.12, s32[1,512]{1,0:T(1,128)} %bitcast.13, f32[32,4096]{1,0:T(8,128)} %bitcast.8, f32[32,128]{1,0:T(8,128)} %bitcast.11), custom_call_target="tpu_custom_call" | custom-call | tf_op jit(solution)/shard_map/pallas_call | solution.py:451
  71.0 1.4 %copy.8 = f32[1,32,256]{2,1,0:T(8,128)} copy(f32[1,32,256]{2,1,0:T(8,128)} %bitcast.9) | data formatting | bytes 65536

commit v7 on v6

--- a/solution.py
+++ b/solution.py
@@ -164,6 +164,8 @@
         range(1, ncol), key=lambda i: -min(i // side, side - i // side) - min(i % side, side - i % side)
     )
 
+    near = ncol // 2
+
     def send(src, dst, send_sem, recv_sem, where):
         pltpu.make_async_remote_copy(
             src_ref=src, dst_ref=dst, send_sem=send_sem, recv_sem=recv_sem, device_id=where, device_id_type=MESH
@@ -288,10 +290,13 @@
 
     def forward(p, u, s, vecs):
         act(mt.at[p], vecs, done.at[s], 2, parts)
-        term[u, s] = placed(ohr[p], joined(done.at[s])).reshape(ncol, nbf, LANES)
-        each_col(
-            lambda i: send(term.at[u, s, i], rs.at[u, s, i], rs_send.at[u, s], rs_recv.at[u, s], (1, r, back_col(i)))
-        )
+        both = joined(done.at[s])
+        for first in (near, 0):
+            part = placed(ohr[p, first * nbf : (first + near) * nbf], both)
+            term[u, s, first : first + near] = part.reshape(near, nbf, LANES)
+            for i in cols_away:
+                if first <= i < first + near:
+                    send(term.at[u, s, i], rs.at[u, s, i], rs_send.at[u, s], rs_recv.at[u, s], (1, r, back_col(i)))
 
     def middle(p, u, s, summed):
         small[0] = stood_up_twice(summed)

time: 72.8 us -> 71.8 us (0.986)
  no operation moved by 1% of the time
where the time goes in v7:
time: 71.8 us; the launch traced here: 71.7 us
  Pallas kernels  70.3 us (98%)
  local copies, waits for them, and re-layouts  1.38 us (2%)
    pallas_call x1, Pallas kernels, per_device(): pl.pallas_call(functools.partial(kernel, nrow, ncol), out_shape=jax.Shape...  70.3 us

profile of v7, /device:TPU:32, one launch (start us, length us, event | category | flops | bytes accessed | tf_op | source)
XLA Modules:
  0.0 71.7 jit_solution(4574883028303877712)
XLA Ops:
  0.0 70.3 %shard_map.64 = f32[32,256]{1,0:T(8,128)} custom-call(f32[32,256]{1,0:T(8,128)} %bitcast.10, f32[512,4096]{1,0:T(8,128)} %bitcast.7, s32[1,512]{1,0:T(1,128)} %bitcast.12, s32[1,512]{1,0:T(1,128)} %bitcast.13, f32[32,4096]{1,0:T(8,128)} %bitcast.8, f32[32,128]{1,0:T(8,128)} %bitcast.11), custom_call_target="tpu_custom_call" | custom-call | tf_op jit(solution)/shard_map/pallas_call | solution.py:456
  70.3 1.4 %copy.8 = f32[1,32,256]{2,1,0:T(8,128)} copy(f32[1,32,256]{2,1,0:T(8,128)} %bitcast.9) | data formatting | bytes 65536

commit v8 on v7

--- a/solution.py
+++ b/solution.py
@@ -455,7 +455,7 @@
     dma = pltpu.SemaphoreType.DMA
     got = pl.pallas_call(
         functools.partial(kernel, nrow, ncol),
-        out_shape=jax.ShapeDtypeStruct((nbf, rhs.shape[2]), F32),
+        out_shape=pltpu.VMEM((nbf, rhs.shape[2]), F32),
         in_specs=[pl.BlockSpec(memory_space=pl.ANY)] * 6,
         out_specs=vm,
         scratch_shapes=[

time: 71.8 us -> 70.4 us (0.981)
  local copies, waits for them, and re-layouts: 1.38 us -> 0.62 us
    unnamed x1, local copies, waits for them, and re-layouts: 1.38 us -> 0.62 us
where the time goes in v8:
time: 70.4 us; the launch traced here: 70.3 us
  Pallas kernels  69.7 us (99%)
    pallas_call x1, Pallas kernels, per_device(): pl.pallas_call(functools.partial(kernel, nrow, ncol), out_shape=pltpu.VME...  69.7 us

profile of v8, /device:TPU:32, one launch (start us, length us, event | category | flops | bytes accessed | tf_op | source)
XLA Modules:
  0.0 70.3 jit_solution(8377385480209928829)
XLA Ops:
  0.0 69.7 %shard_map.64 = f32[32,256]{1,0:T(8,128)S(1)} custom-call(f32[32,256]{1,0:T(8,128)} %bitcast.10, f32[512,4096]{1,0:T(8,128)} %bitcast.8, s32[1,512]{1,0:T(1,128)} %bitcast.12, s32[1,512]{1,0:T(1,128)} %bitcast.13, f32[32,4096]{1,0:T(8,128)} %bitcast.9, f32[32,128]{1,0:T(8,128)} %bitcast.11), custom_call_target="tpu_custom_call" | custom-call | tf_op jit(solution)/shard_map/pallas_call | solution.py:456
  69.7 0.6 copy.8

commit v9 on v8

--- a/solution.py
+++ b/solution.py
@@ -57,7 +57,7 @@
                 outs[t, pl.ds(pl.multiple_of(r * BLOCK + 8 * q, 8), 8), :] = rows
             return 0
 
-        return lax.fori_loop(0, mats.shape[1] // (8 * BLOCK), group, 0)
+        return lax.fori_loop(0, mats.shape[1] // (8 * BLOCK), group, 0, unroll=4 if mats.shape[1] > 8 * BLOCK else 1)
 
     lax.fori_loop(0, mats.shape[0], tile, 0)
 
@@ -77,7 +77,7 @@
             return tuple(sums)
 
         zero = jnp.zeros((8, LANES), F32)
-        sums = lax.fori_loop(0, mats.shape[1] // (8 * BLOCK), group, (zero,) * (8 * count))
+        sums = lax.fori_loop(0, mats.shape[1] // (8 * BLOCK), group, (zero,) * (8 * count), unroll=4 if mats.shape[1] > 8 * BLOCK else 1)
         for r in range(count):
             for g in range(8):
                 outs[t, pl.ds(r * BLOCK + 8 * g, 8), :] = sums[r * 8 + g]

time: 70.4 us -> 69.2 us (0.983)
  Pallas kernels: 69.7 us -> 68.5 us
    pallas_call x1, Pallas kernels: 69.7 us -> 68.5 us  [per_device(): pl.pallas_call(functools.partial(kernel, nrow, ncol), out_shape=pltpu.VME...]
where the time goes in v9:
time: 69.2 us; the launch traced here: 69.1 us
  Pallas kernels  68.5 us (99%)
    pallas_call x1, Pallas kernels, per_device(): pl.pallas_call(functools.partial(kernel, nrow, ncol), out_shape=pltpu.VME...  68.5 us

profile of v9, /device:TPU:32, one launch (start us, length us, event | category | flops | bytes accessed | tf_op | source)
XLA Modules:
  0.0 69.1 jit_solution(3566618931388502477)
XLA Ops:
  0.0 68.5 %shard_map.64 = f32[32,256]{1,0:T(8,128)S(1)} custom-call(f32[32,256]{1,0:T(8,128)} %bitcast.10, f32[512,4096]{1,0:T(8,128)} %bitcast.8, s32[1,512]{1,0:T(1,128)} %bitcast.12, s32[1,512]{1,0:T(1,128)} %bitcast.13, f32[32,4096]{1,0:T(8,128)} %bitcast.9, f32[32,128]{1,0:T(8,128)} %bitcast.11), custom_call_target="tpu_custom_call" | custom-call | tf_op jit(solution)/shard_map/pallas_call | solution.py:456
  68.5 0.6 copy.8
